TPU v7x, 128 devices: a whole 4x4x4 slice. The times are simulated.
128 devices in a mesh: shard: 8 (over z, core), replica: 16 (over y, x).
Axes of the slice: x: 4, y: 4, z: 4, core: 2. Of those that a mesh axis runs over, the one named last changes fastest.
Arguments:
- partial_grads: bfloat16 [16, 128, 512, 512], P('replica', 'shard'), may hold values from -64 to 64
- owner_list: int32 [128, 1], replicated, may hold values from 0 to 15; in each aligned block of 16 rows (0 to 15, 16 to 31, ...) at most 2 rows name the same one
- left_stat: float32 [8, 16, 2, 512, 512], P('shard', 'replica'), may hold values from -1 to 5, as said below
- right_stat: float32 [8, 16, 2, 512, 512], P('shard', 'replica'), may hold values from -1 to 5, as said below
- left_root: float32 [8, 16, 2, 512, 512], P('shard', 'replica'), may hold values from -1 to 2, as said below
- right_root: float32 [8, 16, 2, 512, 512], P('shard', 'replica'), may hold values from -1 to 2, as said below
Outputs:
- update: bfloat16 [128, 512, 512], P(('shard', 'replica'))
- left_new: float32 [8, 16, 2, 512, 512], P('shard', 'replica')
- right_new: float32 [8, 16, 2, 512, 512], P('shard', 'replica')
Inputs may be any that keep to these rules, and one draw needn't show every extreme that they name: `owner_list`: among the 16 blocks of one column no owner is named more than 2 times, a bound that some block reaches. `left_stat`: Symmetric. `right_stat`: Symmetric. `left_root`: Symmetric. `right_root`: Symmetric.
All inputs are finite; a program needn't handle non-finite values.
Results may differ from a plain program's by a relative error of at most 0.02.
Values may be sent and summed in bfloat16 or wider, within the bound.
A program may use at most 128 MiB of HBM per device.

v0:
```python
import jax
import jax.numpy as jnp
from jax import lax
from jax.sharding import PartitionSpec as P

decay_keep = 0.9
epsilon = 1e-06
rms_limit = 0.5


def on_device(partial_grads, owner_list, left_stat, right_stat, left_root, right_root):
    rep_count = lax.axis_size("replica")
    shard_count = lax.axis_size("shard")
    column = lax.axis_index("shard")
    own_index = lax.axis_index("replica")
    slots_cap = left_stat.shape[2]
    block_size = left_stat.shape[3]
    local_terms = partial_grads[0]
    owners = lax.dynamic_slice_in_dim(owner_list[:, 0], column * rep_count, rep_count)
    position = lax.iota(jnp.int32, rep_count)
    same_owner = owners[:, None] == owners[None, :]
    earlier = position[None, :] < position[:, None]
    slot_index = jnp.sum((same_owner & earlier).astype(jnp.int32), axis=1)
    slot_ids = lax.iota(jnp.int32, slots_cap)
    chosen = (owners[None, :] == own_index) & (slot_index[None, :] == slot_ids[:, None])
    chosen_bf = chosen.astype(jnp.bfloat16)
    summed = lax.psum_scatter(
        local_terms.astype(jnp.float32).astype(jnp.bfloat16),
        "replica",
        scatter_dimension=0,
        tiled=True,
    )
    gradient = jnp.einsum(
        "kj,jab->kab",
        chosen_bf,
        lax.all_gather(summed, "replica", axis=0, tiled=True),
        preferred_element_type=jnp.float32,
    ).astype(jnp.bfloat16)
    filled = jnp.any(chosen, axis=1)[:, None, None]
    left_old = left_stat[0, 0]
    right_old = right_stat[0, 0]
    left_prod = jnp.einsum("kab,kcb->kac", gradient, gradient, preferred_element_type=jnp.float32)
    right_prod = jnp.einsum("kba,kbc->kac", gradient, gradient, preferred_element_type=jnp.float32)
    left_new = jnp.where(
        filled, decay_keep * left_old + (1.0 - decay_keep) / block_size * left_prod, left_old
    )
    right_new = jnp.where(
        filled, decay_keep * right_old + (1.0 - decay_keep) / block_size * right_prod, right_old
    )
    grad_wide = gradient.astype(jnp.float32)
    precond = jnp.einsum(
        "kab,kbc->kac", left_root[0, 0], grad_wide, precision=lax.Precision.HIGHEST
    )
    precond = jnp.einsum("kab,kbc->kac", precond, right_root[0, 0], precision=lax.Precision.HIGHEST)
    graft = jnp.sqrt(jnp.mean(grad_wide * grad_wide, axis=(1, 2)) + epsilon) / jnp.sqrt(
        jnp.mean(precond * precond, axis=(1, 2)) + epsilon
    )
    total_sq = lax.psum(jnp.sum(grad_wide * grad_wide), ("shard", "replica"))
    grad_rms = jnp.sqrt(total_sq / (shard_count * rep_count * block_size * block_size))
    clip_scale = jnp.minimum(1.0, rms_limit / grad_rms)
    ready = (precond * graft[:, None, None] * clip_scale).astype(jnp.bfloat16)
    flat_target = owners[own_index] * slots_cap + slot_index[own_index]
    block_piece = lax.all_gather(ready, "replica", axis=0, tiled=True)
    flat_here = lax.iota(jnp.int32, block_piece.shape[0])
    weight = (flat_here == flat_target).astype(jnp.bfloat16)
    back = jnp.einsum("p,pab->ab", weight, block_piece, preferred_element_type=jnp.float32)[None]
    update = back.astype(jnp.bfloat16)
    return (update, left_new[None, None], right_new[None, None])


def solution(mesh):
    return jax.shard_map(
        on_device,
        mesh=mesh,
        in_specs=(
            P("replica", "shard", None, None),
            P(),
            P("shard", "replica", None, None, None),
            P("shard", "replica", None, None, None),
            P("shard", "replica", None, None, None),
            P("shard", "replica", None, None, None),
        ),
        out_specs=(
            P(("shard", "replica"), None, None),
            P("shard", "replica", None, None, None),
            P("shard", "replica", None, None, None),
        ),
        check_vma=False,
    )
```

profile of v0, /device:TPU:0, one launch (start us, length us, event | category | flops | bytes accessed | tf_op | source)
XLA Modules:
  0.0 392.3 jit_solution(11117497720094095330)
XLA Ops:
  7.2 0.0 copy-start
  7.2 0.0 reduce-scatter.4.cloned.1.call-start
  7.2 0.0 copy-start.3
  7.2 0.7 reduce-scatter.4.cloned.1.call-update
  7.9 0.0 all-gather.3.cloned.1.call-start
  8.0 91.1 %reduce-scatter.4.cloned.1.call-done = bf16[1,512,512]{2,1,0:T(8,128)(2,1)} async-done(((bf16[16,512,512]{2,1,0:T(8,128)(2,1)}), bf16[1,512,512]{2,1,0:T(8,128)(2,1)}) %reduce-scatter.4.cloned.1.call-update) | async-done | bytes 524304
  99.0 0.0 all-gather.3.cloned.1.call-update
  99.0 0.0 all-gather.5.cloned.1.call-start
  99.1 0.0 copy-done.3
  99.1 0.1 broadcast_compare_fusion
  99.2 0.2 convert_reduce_fusion
  99.4 71.9 %all-gather.3.cloned.1.call-done = bf16[16,512,512]{2,1,0:T(8,128)(2,1)} async-done(((bf16[1,512,512]{2,1,0:T(8,128)(2,1)}), bf16[16,512,512]{2,1,0:T(8,128)(2,1)}) %all-gather.3.cloned.1.call-update) | async-done | bytes 8388624 | tf_op jit(solution)/shard_map/all_gather | solution.py:36
  171.3 10.2 %fusion.13 = (f32[2]{0:T(128)S(1)}, f32[]{:T(128)}, bf16[2,512,512]{2,0,1:T(2,128)(2,1)}) fusion(bf16[16,512,512]{2,1,0:T(8,128)(2,1)} %all-gather.3.cloned.1.call-done, pred[16]{0:T(512)(128)(4,1)S(1)} %get-tuple-element.5, s32[16]{0:T(128)S(1)} %convert_reduce_fusion), kind=kOutput, calls=%fused_computation.20 | convolution fusion | flops 19398716 | bytes 9437276 | tf_op jit(solution)/shard_map/kj,jab->kab/dot_general | solution.py:33
  181.4 2.4 copy.20
  183.9 64.9 %psum.7 = f32[]{:T(128)} all-reduce(f32[]{:T(128)} %get-tuple-element.4), channel_id=1, replica_groups=mesh['shard'=8,'replica'=16] {'shard','replica'}, use_global_device_ids=true, to_apply=%region_5.6 | all-reduce | flops 1 | bytes 8 | tf_op jit(solution)/shard_map/psum | solution.py:58
  249.5 3.4 fusion.10
  252.9 0.0 copy-done
  252.9 4.8 %multiply_reduce_fusion = (f32[2]{0:T(128)S(1)}, f32[2,512,512]{2,1,0:T(8,128)}) fusion(f32[2,512,512]{1,2,0:T(8,128)S(1)} %fusion.10, f32[1,1,2,512,512]{4,3,2,1,0:T(8,128)S(1)} %copy-done), kind=kOutput, calls=%fused_computation.17 | convolution fusion | flops 3222274048 | bytes 6291464 | tf_op jit(solution)/shard_map/kab,kbc->kac/dot_general | solution.py:54
  257.8 3.0 multiply_convert_fusion
  260.7 0.0 all-gather.5.cloned.1.call-update
  260.7 0.6 dynamic_slice.14
  261.3 0.6 fusion.29
  263.2 0.1 fusion.24
  263.3 0.0 copy-start.1
  263.3 0.0 copy-start.2
  263.3 4.6 %fusion.7 = f32[1,1,2,512,512]{4,3,2,1,0:T(8,128)} fusion(f32[1,1,2,512,512]{4,3,2,1,0:T(8,128)} %param.8, pred[2]{0:T(512)(128)(4,1)S(1)} %fusion.24, bf16[2,512,512]{2,0,1:T(2,128)(2,1)} %get-tuple-element.7), kind=kOutput, calls=%fused_computation.11 | convolution fusion | flops 538968064 | bytes 5242882 | tf_op jit(solution)/shard_map/kab,kcb->kac/dot_general | solution.py:42
  268.0 0.0 copy-done.1
  268.0 0.0 copy-done.2
  268.0 2.2 fusion.5
  270.1 99.2 %all-gather.5.cloned.1.call-done = bf16[32,512,512]{2,1,0:T(8,128)(2,1)} async-done(((bf16[2,512,512]{2,1,0:T(8,128)(2,1)}), bf16[32,512,512]{2,1,0:T(8,128)(2,1)}) %all-gather.5.cloned.1.call-update) | async-done | bytes 16777232 | tf_op jit(solution)/shard_map/all_gather | solution.py:63
  369.3 15.5 %fusion = bf16[1,512,512]{2,0,1:T(2,128)(2,1)S(1)} fusion(bf16[32,512,512]{2,1,0:T(8,128)(2,1)} %all-gather.5.cloned.1.call-done, s32[]{:T(128)S(6)} %add.38), kind=kOutput, calls=%fused_computation | convolution fusion | flops 16777248 | bytes 17301508 | tf_op jit(solution)/shard_map/p,pab->ab/dot_general | solution.py:66
  384.8 0.9 copy.44
  (1 shorter events, 0.0 us)
Async XLA Ops:
  7.2 245.7 %copy-start = (f32[1,1,2,512,512]{4,3,2,1,0:T(8,128)S(1)}, f32[1,1,2,512,512]{4,3,2,1,0:T(8,128)}, u32[]{:S(2)}) copy-start(f32[1,1,2,512,512]{4,3,2,1,0:T(8,128)} %param.11) | copy-start | bytes 6291460
  7.2 91.8 %reduce-scatter.4.cloned.1.call-start = ((), (), s32[]{:S(2)}) async-start(), calls=%async_computation.3 | async-start | bytes 8912896
  7.2 91.9 %copy-start.3 = (s32[128,1]{0,1:T(1,128)S(1)}, s32[128,1]{0,1:T(1,128)}, u32[]{:S(2)}) copy-start(s32[128,1]{0,1:T(1,128)} %param.7) | copy-start | bytes 1540
  7.9 163.4 %all-gather.3.cloned.1.call-start = ((), (), s32[]{:S(2)}) async-start(), calls=%async_computation.1 | async-start | bytes 8912896 | tf_op jit(solution)/shard_map/all_gather | solution.py:36
  99.0 270.3 %all-gather.5.cloned.1.call-start = ((), (), s32[]{:S(2)}) async-start(), calls=%async_computation.2 | async-start | bytes 17825792 | tf_op jit(solution)/shard_map/all_gather | solution.py:63
  263.3 4.6 %copy-start.1 = (bf16[2,512,512]{2,0,1:T(2,128)(2,1)S(1)}, bf16[2,512,512]{2,0,1:T(2,128)(2,1)}, u32[]{:S(2)}) copy-start(bf16[2,512,512]{2,0,1:T(2,128)(2,1)} %get-tuple-element.7) | copy-start | bytes 3145732
  263.3 4.6 %copy-start.2 = (f32[1,1,2,512,512]{4,3,2,1,0:T(8,128)S(1)}, f32[1,1,2,512,512]{4,3,2,1,0:T(8,128)}, u32[]{:S(2)}) copy-start(f32[1,1,2,512,512]{4,3,2,1,0:T(8,128)} %param.9) | copy-start | bytes 6291460
Sparse Core Ops, SparseCore 0:
  11.4 87.5 reduce-scatter.3
  101.2 70.0 all-gather.2
  260.9 108.4 all-gather.4
where the time goes:
time: 393 us; the launch traced here: 392 us
  waiting for transfers between devices  263 us (67%)
  blocking collectives  64.9 us (17%)
  matrix products  40.7 us (10%)
  between operations  15.8 us (4%)
  local copies, waits for them, and re-layouts  3.97 us (1%)
  other arithmetic  3.93 us (1%)
    all_gather x1, waiting for transfers between devices, on_device(): block_piece = lax.all_gather(ready, 'replica', axis=0, tiled=True)  99.2 us
    unnamed x4, waiting for transfers between devices  91.8 us
    all_gather x1, waiting for transfers between devices, on_device(): lax.all_gather(summed, 'replica', axis=0, tiled=True)  71.9 us
    psum x1, blocking collectives, on_device(): total_sq = lax.psum(jnp.sum(grad_wide * grad_wide), ('shard', 'replica'))  64.9 us
    dot_general x1, matrix products, on_device(): jnp.einsum('p,pab->ab', weight, block_piece, preferred_element_type=jnp.f...  15.5 us
    dot_general x1, matrix products, on_device(): jnp.einsum('kj,jab->kab', chosen_bf, lax.all_gather(summed, 'replica', ax...  10.2 us
  transfers between devices with their start and end apart: 3, of which 3 were waited for; matrix products, arithmetic and copies ran while one was open for 2% of the time, Pallas kernels for 0%

commit v1 on v0

v1 whole, which is shorter than its diff:
```python
import functools

import jax
import jax.numpy as jnp
from jax import lax
from jax.experimental import pallas as pl
from jax.experimental.pallas import tpu as pltpu
from jax.sharding import PartitionSpec as P

decay_keep = 0.9
epsilon = 1e-06
rms_limit = 0.5

MESH = pl.DeviceIdType.MESH
f32 = jnp.float32
bf16 = jnp.bfloat16

SIDE = 4
REPS = 16
COLS = 8
SLOTS = 2
BLOCK = 512
PIECE = 32
HALF = 16
WIDE = 256
STEPS = BLOCK // WIDE


def kernel(
    grads, owners, left_stat, right_stat, left_root, right_root,
    update, left_out, right_out,
    far_in, near_in, both_in, near_own, last_own, line_sum, line_in, piece,
    to_owner, block_in, root_in, root_hi, root_lo, stat_in, precond, ready,
    held_first, held_last, to_place, squares, squares_in, table,
    load_sem, root_sem, stat_sem, out_sem, own_sem,
    far_s, far_r, near_s, near_r, both_s, both_r, line_s, line_r,
    owner_s, owner_r, held_s, held_r, place_s, place_r,
    zsum_s, zsum_r, psum_s, psum_r,
):
    s = lax.axis_index("shard")
    r = lax.axis_index("replica")
    x, y = r % SIDE, r // SIDE

    def along(half, step):
        if half == 0:
            return (s, y * SIDE + (x + step) % SIDE)
        return (s, (y + step) % SIDE * SIDE + x)

    def send(src, dst, send_sem, recv_sem, device):
        return pltpu.make_async_remote_copy(
            src_ref=src, dst_ref=dst, send_sem=send_sem, recv_sem=recv_sem,
            device_id=device, device_id_type=MESH,
        )

    def chunk(half, step, first, count, wide):
        place = ((x if half == 0 else y) + step) % SIDE
        rows = pl.ds(first, count)
        cols = pl.ds(wide * WIDE, WIDE)
        if half == 0:
            return grads.at[rows, :, place, 0, :, cols]
        return grads.at[rows, place, :, 1, :, cols]

    barrier = pltpu.get_barrier_semaphore()

    @pl.loop(1, REPS)
    def _(d):
        pl.semaphore_signal(barrier, inc=1, device_id=(s, (r + d) % REPS), device_id_type=MESH)

    @pl.loop(1, COLS)
    def _(d):
        pl.semaphore_signal(barrier, inc=1, device_id=((s + d) % COLS, r), device_id_type=MESH)

    pl.semaphore_wait(barrier, REPS + COLS - 2)

    held = (held_first, held_last)
    groups = [(wide, half) for wide in range(STEPS) for half in range(2)]

    def far(g, way):
        wide, half = groups[g]
        return send(chunk(half, 2, 8 * way, 8, wide), far_in.at[g, way],
                    far_s.at[g, way], far_r.at[g, way], along(half, 1 - 2 * way))

    def near(g, way):
        wide, half = groups[g]
        return send(chunk(half, 1 - 2 * way, 8 - 8 * way, 8, wide), near_in.at[g, way],
                    near_s.at[g, way], near_r.at[g, way], along(half, 1 - 2 * way))

    def both(g, way):
        wide, half = groups[g]
        return send(near_own.at[g, way], both_in.at[g, way],
                    both_s.at[g, way], both_r.at[g, way], along(half, 1 - 2 * way))

    def line(g, d):
        wide, half = groups[g]
        place = ((y if half == 0 else x) + d) % SIDE
        return send(line_sum.at[g, place], line_in.at[g, d - 1],
                    line_s.at[g, d - 1], line_r.at[g, d - 1], along(1 - half, d))

    def load_near(g, way):
        wide, half = groups[g]
        return pltpu.make_async_copy(chunk(half, 1 - 2 * way, 8 * way, 8, wide),
                                     near_own.at[g, way], load_sem.at[g, way])

    def load_last(g):
        wide, half = groups[g]
        return pltpu.make_async_copy(chunk(half, 0, 0, REPS, wide),
                                     last_own.at[g], load_sem.at[g, 2])

    for g in range(len(groups)):
        for way in range(2):
            far(g, way).start()
            load_near(g, way).start()
        load_last(g).start()
        for way in range(2):
            near(g, way).start()

    roots = [pltpu.make_async_copy(ref, root_in.at[i], root_sem.at[i])
             for i, ref in enumerate((left_root, right_root))]
    stats = [pltpu.make_async_copy(ref, stat_in.at[i], stat_sem.at[i])
             for i, ref in enumerate((left_stat, right_stat))]
    for copy in roots + stats:
        copy.start()

    @pl.loop(0, REPS)
    def _(j):
        mine = owners[0, s * REPS + j]
        count = jnp.int32(0)
        for i in range(REPS):
            hit = (owners[0, s * REPS + i] == mine) & (i < j)
            count = count + hit.astype(jnp.int32)
        table[1, j] = mine
        table[2, j] = jnp.minimum(count, SLOTS - 1)

    @pl.loop(0, REPS)
    def _(o):
        first, second = jnp.int32(REPS), jnp.int32(REPS)
        for j in range(REPS):
            hit = table[1, j] == o
            first = jnp.where(hit & (table[2, j] == 0), j, first)
            second = jnp.where(hit & (table[2, j] == 1), j, second)
        table[0, o * SLOTS] = first
        table[0, o * SLOTS + 1] = second

    for wide in range(STEPS):
        piece[wide, REPS] = jnp.zeros((PIECE, WIDE), bf16)

    for copy in roots:
        copy.wait()

    @pl.loop(0, 2 * SLOTS * 8)
    def _(i):
        side, k, t = i // (SLOTS * 8), i // 8 % SLOTS, i % 8
        rows = pl.ds(pl.multiple_of(t * 64, 64), 64)
        whole = root_in[side, k, rows, :]
        top = whole.astype(bf16)
        root_hi[side, k, rows, :] = top
        root_lo[side, k, rows, :] = (whole - top.astype(f32)).astype(bf16)

    squares[...] = jnp.zeros_like(squares)

    def combine(g):
        for way in range(2):
            load_near(g, way).wait()
            far(g, way).wait_recv()

            @pl.loop(0, 8)
            def _(b):
                near_own[g, way, b] = near_own[g, way, b] + far_in[g, way, b]

            both(g, way).start()

    def line_total(g):
        load_last(g).wait()
        for way in range(2):
            near(g, way).wait_recv()
            both(g, way).wait_recv()

        @pl.loop(0, 8)
        def _(b):
            for way in range(2):
                total = (last_own[g, 8 * way + b].astype(f32)
                         + both_in[g, way, b].astype(f32)
                         + near_in[g, 1 - way, b].astype(f32))
                line_sum[g, :, 8 * way + b] = total.astype(bf16)

        for d in (2, 1, 3):
            line(g, d).start()

    def total(g):
        wide, half = groups[g]
        for d in (1, 2, 3):
            line(g, d).wait_recv()
        place = y if half == 0 else x

        @pl.loop(0, REPS)
        def _(b):
            value = line_sum[g, place, b].astype(f32)
            for d in range(3):
                value = value + line_in[g, d, b].astype(f32)
            value = value.astype(bf16)
            piece[wide, b, pl.ds(half * HALF, HALF), :] = value
            value = value.astype(f32)
            value = value * value
            value = value[:, :128] + value[:, 128:]
            squares[0] += value[:8] + value[8:]

    def owner(wide, d):
        return send(to_owner.at[wide, (r + d) % REPS], block_in.at[wide, :, r],
                    owner_s.at[wide, d], owner_r.at[wide, d], (s, (r + d) % REPS))

    def route(wide):
        @pl.loop(0, REPS)
        def _(o):
            for k in range(SLOTS):
                to_owner[wide, o, k] = piece[wide, table[0, o * SLOTS + k]]

        @pl.loop(1, REPS)
        def _(d):
            owner(wide, d).start()

        block_in[wide, :, r] = to_owner[wide, r]

    def wait_route(wide):
        @pl.loop(1, REPS)
        def _(d):
            owner(wide, d).wait_recv()

    def product(wide):
        @pl.loop(0, SLOTS * 2)
        def _(i):
            k, t = i // 2, i % 2
            rows = pl.ds(pl.multiple_of(t * 256, 256), 256)
            block = block_in[wide, k].reshape(BLOCK, WIDE)
            part = (jnp.dot(root_hi[0, k, rows, :], block, preferred_element_type=f32)
                    + jnp.dot(root_lo[0, k, rows, :], block, preferred_element_type=f32))
            top = part.astype(bf16)
            low = (part - top.astype(f32)).astype(bf16)
            across = pl.ds(wide * WIDE, WIDE)
            hi, lo = root_hi[1, k, across, :], root_lo[1, k, across, :]
            value = (jnp.dot(top, hi, preferred_element_type=f32)
                     + jnp.dot(top, lo, preferred_element_type=f32)
                     + jnp.dot(low, hi, preferred_element_type=f32))
            if wide == 0:
                precond[k, rows, :] = value
            else:
                precond[k, rows, :] += value

    combine(0)
    combine(1)
    combine(2)
    combine(3)
    line_total(0)
    line_total(1)
    total(0)
    total(1)
    route(0)
    line_total(2)
    line_total(3)
    total(2)
    total(3)
    route(1)

    def zsum(d):
        return send(squares.at[0], squares_in.at[d], zsum_s.at[d], zsum_r.at[d], ((s + d) % COLS, r))

    def psum(d):
        return send(squares.at[1], squares_in.at[COLS + d], psum_s.at[d], psum_r.at[d], (s, (r + d) % REPS))

    for d in range(1, COLS):
        zsum(d).start()

    wait_route(0)
    product(0)

    column = squares[0]
    for d in range(1, COLS):
        zsum(d).wait_recv()
        column = column + squares_in[d]
    squares[1] = column

    @pl.loop(1, REPS)
    def _(d):
        psum(d).start()

    wait_route(1)
    product(1)

    def hold(wide, d):
        return send(ready.at[wide, :, (r + d) % REPS], held[wide].at[r],
                    held_s.at[wide, d], held_r.at[wide, d], (s, (r + d) % REPS))

    scales = []
    for k in range(SLOTS):
        def square_sum(i, carry):
            value, power = carry
            across = pl.ds(pl.multiple_of(i * PIECE, PIECE), PIECE)
            p = precond[k, across, :]
            power = power + p * p
            for wide in range(STEPS):
                g = block_in[wide, k, i].astype(f32)
                value = value + g * g
            return value, power

        value, power = lax.fori_loop(
            0, REPS, square_sum, (jnp.zeros((PIECE, WIDE), f32), jnp.zeros((PIECE, BLOCK), f32)))
        value = jnp.sum(value, axis=(0, 1), keepdims=True) / (BLOCK * BLOCK)
        power = jnp.sum(power, axis=(0, 1), keepdims=True) / (BLOCK * BLOCK)
        scales.append(jnp.sqrt(value + epsilon) / jnp.sqrt(power + epsilon))

    all_squares = squares[1]
    for d in range(1, REPS):
        psum(d).wait_recv()
        all_squares = all_squares + squares_in[COLS + d]
    rms = jnp.sqrt(jnp.sum(all_squares, axis=(0, 1), keepdims=True)
                   / (COLS * REPS * BLOCK * BLOCK))
    clip = jnp.minimum(1.0, rms_limit / rms)

    scales = [scale * clip for scale in scales]

    for wide in range(STEPS):
        for k in range(SLOTS):
            @pl.loop(0, REPS)
            def _(i):
                across = pl.ds(pl.multiple_of(i * PIECE, PIECE), PIECE)
                value = precond[k, across, pl.ds(wide * WIDE, WIDE)] * scales[k]
                ready[wide, k, i] = value.astype(bf16)

        @pl.loop(1, REPS)
        def _(d):
            hold(wide, d).start()

        held[wide][r] = ready[wide, :, r]

    for copy in stats:
        copy.wait()

    @pl.loop(0, SLOTS)
    def _(k):
        filled = table[0, r * SLOTS + k] < REPS
        keep = jnp.where(filled, decay_keep, 1.0).astype(f32)
        weight = (1.0 - decay_keep) / BLOCK
        for t in range(2):
            rows = pl.ds(t * 256, 256)
            left = jnp.zeros((256, BLOCK), f32)
            for wide in range(STEPS):
                block = block_in[wide, k].reshape(BLOCK, WIDE)
                left = left + lax.dot_general(
                    block[t * 256:(t + 1) * 256], block, (((1,), (1,)), ((), ())),
                    preferred_element_type=f32)
            stat_in[0, k, rows, :] = keep * stat_in[0, k, rows, :] + weight * left
            for wide in range(STEPS):
                across = pl.ds(wide * WIDE, WIDE)
                right = lax.dot_general(
                    block_in[t, k].reshape(BLOCK, WIDE), block_in[wide, k].reshape(BLOCK, WIDE),
                    (((0,), (0,)), ((), ())), preferred_element_type=f32)
                stat_in[1, k, rows, across] = keep * stat_in[1, k, rows, across] + weight * right

    outs = [pltpu.make_async_copy(stat_in.at[i], ref, out_sem.at[i])
            for i, ref in enumerate((left_out, right_out))]
    for copy in outs:
        copy.start()

    def settle(wide, d):
        return send(to_place.at[wide, (r + d) % REPS], update.at[r, :, pl.ds(wide * WIDE, WIDE)],
                    place_s.at[wide, d], place_r.at[wide, d], (s, (r + d) % REPS))

    own = []
    for wide in range(STEPS):
        @pl.loop(1, REPS)
        def _(d):
            hold(wide, d).wait_recv()

        @pl.loop(0, REPS)
        def _(j):
            to_place[wide, j] = held[wide][table[1, j], table[2, j]]

        @pl.loop(1, REPS)
        def _(d):
            settle(wide, d).start()

        own.append(pltpu.make_async_copy(
            to_place.at[wide, r], update.at[r, :, pl.ds(wide * WIDE, WIDE)], own_sem.at[wide]))
        own[-1].start()

    for g in range(len(groups)):
        for way in range(2):
            far(g, way).wait_send()
            near(g, way).wait_send()
            both(g, way).wait_send()
        for d in (1, 2, 3):
            line(g, d).wait_send()
    for d in range(1, COLS):
        zsum(d).wait_send()
    for copy in outs + own:
        copy.wait()

    @pl.loop(1, REPS)
    def _(d):
        psum(d).wait_send()
        for wide in range(STEPS):
            owner(wide, d).wait_send()
            hold(wide, d).wait_send()
            settle(wide, d).wait_send()
            settle(wide, d).wait_recv()


def on_device(partial_grads, owner_list, left_stat, right_stat, left_root, right_root):
    grads = partial_grads.reshape(REPS, SIDE, SIDE, 2, HALF, BLOCK)
    any_spec = pl.BlockSpec(memory_space=pl.ANY)
    dma = pltpu.SemaphoreType.DMA
    groups = 2 * STEPS
    pair = [dma((groups, 2))] * 2
    ring = [dma((STEPS, REPS))] * 2
    state = jax.ShapeDtypeStruct((SLOTS, BLOCK, BLOCK), f32)
    update, left_new, right_new = pl.pallas_call(
        kernel,
        out_shape=(
            jax.ShapeDtypeStruct((REPS, PIECE, BLOCK), bf16),
            state,
            state,
        ),
        in_specs=[any_spec, pl.BlockSpec(memory_space=pltpu.SMEM)] + [any_spec] * 4,
        out_specs=(any_spec, any_spec, any_spec),
        scratch_shapes=[
            pltpu.VMEM((groups, 2, 8, SIDE, HALF, WIDE), bf16),
            pltpu.VMEM((groups, 2, 8, SIDE, HALF, WIDE), bf16),
            pltpu.VMEM((groups, 2, 8, SIDE, HALF, WIDE), bf16),
            pltpu.VMEM((groups, 2, 8, SIDE, HALF, WIDE), bf16),
            pltpu.VMEM((groups, REPS, SIDE, HALF, WIDE), bf16),
            pltpu.VMEM((groups, SIDE, REPS, HALF, WIDE), bf16),
            pltpu.VMEM((groups, 3, REPS, HALF, WIDE), bf16),
            pltpu.VMEM((STEPS, REPS + 1, PIECE, WIDE), bf16),
            pltpu.VMEM((STEPS, REPS, SLOTS, PIECE, WIDE), bf16),
            pltpu.VMEM((STEPS, SLOTS, REPS, PIECE, WIDE), bf16),
            pltpu.VMEM((2, SLOTS, BLOCK, BLOCK), f32),
            pltpu.VMEM((2, SLOTS, BLOCK, BLOCK), bf16),
            pltpu.VMEM((2, SLOTS, BLOCK, BLOCK), bf16),
            pltpu.VMEM((2, SLOTS, BLOCK, BLOCK), f32),
            pltpu.VMEM((SLOTS, BLOCK, BLOCK), f32),
            pltpu.VMEM((STEPS, SLOTS, REPS, PIECE, WIDE), bf16),
            pltpu.VMEM((REPS, SLOTS, PIECE, WIDE), bf16),
            pltpu.VMEM((REPS, SLOTS, PIECE, WIDE), bf16),
            pltpu.VMEM((STEPS, REPS, PIECE, WIDE), bf16),
            pltpu.VMEM((2, 8, 128), f32),
            pltpu.VMEM((COLS + REPS, 8, 128), f32),
            pltpu.SMEM((3, REPS * SLOTS), jnp.int32),
            dma((groups, 3)), dma((2,)), dma((2,)), dma((2,)), dma((STEPS,)),
        ] + pair + pair + pair + [dma((groups, 3))] * 2 + ring + ring + ring
        + [dma((COLS,))] * 2 + [dma((REPS,))] * 2,
        compiler_params=pltpu.CompilerParams(
            collective_id=0, has_side_effects=True, vmem_limit_bytes=58 << 20),
    )(grads, owner_list.reshape(1, COLS * REPS), left_stat[0, 0], right_stat[0, 0], left_root[0, 0], right_root[0, 0])
    return (update.reshape(1, BLOCK, BLOCK), left_new[None, None], right_new[None, None])


def solution(mesh):
    return jax.shard_map(
        on_device,
        mesh=mesh,
        in_specs=(
            P("replica", "shard", None, None),
            P(),
            P("shard", "replica", None, None, None),
            P("shard", "replica", None, None, None),
            P("shard", "replica", None, None, None),
            P("shard", "replica", None, None, None),
        ),
        out_specs=(
            P(("shard", "replica"), None, None),
            P("shard", "replica", None, None, None),
            P("shard", "replica", None, None, None),
        ),
        check_vma=False,
    )
```

time: 393 us -> 111 us (0.28)
  waiting for transfers between devices: 263 us -> 0 us
  Pallas kernels: 0 us -> 104 us
  blocking collectives: 64.9 us -> 0 us
  matrix products: 40.7 us -> 0 us
  between operations: 15.8 us -> 0.64 us
  other arithmetic: 3.93 us -> 0 us
    all_gather x2 -> x0, waiting for transfers between devices: 171 us -> none  [the longest x1 99.2 us: on_device(): block_piece = lax.all_gather(ready, 'replica', axis=0, tiled=True)]
    pallas_call x0 -> x1, Pallas kernels: none -> 104 us  [on_device(): pl.pallas_call(kernel, out_shape=(jax.ShapeDtypeStruct((REPS, PIECE, BLOC...]
    unnamed x4 -> x0, waiting for transfers between devices: 91.8 us -> none
    psum x1 -> x0, blocking collectives: 64.9 us -> none  [on_device(): total_sq = lax.psum(jnp.sum(grad_wide * grad_wide), ('shard', 'replica'))]
    dot_general x6 -> x0, matrix products: 40.7 us -> none  [the longest x1 15.5 us: on_device(): jnp.einsum('p,pab->ab', weight, block_piece, preferred_element_type=jnp.f...]
    unnamed x8 -> x5, local copies, waits for them, and re-layouts: 0.02 us -> 6.42 us
  transfers between devices with their start and end apart: 3 -> 0, of which waited for: 3 -> 0; matrix products, arithmetic and copies ran while one was open for 2% -> 0% of each run, Pallas kernels for 0% -> 0%
where the time goes in v1:
time: 111 us
  Pallas kernels  104 us (94%)
  local copies, waits for them, and re-layouts  6.42 us (6%)
    pallas_call x1, Pallas kernels, on_device(): pl.pallas_call(kernel, out_shape=(jax.ShapeDtypeStruct((REPS, PIECE, BLOC...  104 us
    unnamed x5, local copies, waits for them, and re-layouts  6.42 us

profile of v1, /device:TPU:0, one launch (start us, length us, event | category | flops | bytes accessed | tf_op | source)
XLA Modules:
  0.0 111.0 jit_solution(16682048272971208191)
XLA Ops:
  0.6 103.9 %shard_map.85 = (bf16[16,32,512]{2,1,0:T(8,128)(2,1)}, f32[2,512,512]{2,1,0:T(8,128)}, f32[2,512,512]{2,1,0:T(8,128)}) custom-call(bf16[16,4,4,2,16,512]{5,4,3,2,1,0:T(8,128)(2,1)} %bitcast.9, s32[1,128]{1,0:T(1,128)} %bitcast.17, f32[2,512,512]{2,1,0:T(8,128)} %bitcast.10, f32[2,512,512]{2,1,0:T(8,128)} %bitcast.11, f32[2,512,512]{2,1,0:T(8,128)} %bitcast.12, ...), custom_call_target="tpu_custom_call" | custom-call | tf_op jit(solution)/shard_map/pallas_call | solution.py:415
  104.5 1.9 %copy.12 = bf16[1,512,512]{2,1,0:T(8,128)(2,1)} copy(bf16[1,512,512]{2,1,0:T(8,128)(2,1)} %bitcast.16) | data formatting | bytes 1048576
  106.4 0.0 copy-start
  106.4 3.2 %copy.13 = f32[1,1,2,512,512]{4,3,2,1,0:T(8,128)} copy(f32[1,1,2,512,512]{4,3,2,1,0:T(8,128)} %bitcast.15) | data formatting | bytes 4194304
  109.6 0.0 copy-done
  109.6 1.3 %copy.14 = f32[1,1,2,512,512]{4,3,2,1,0:T(8,128)} copy(f32[1,1,2,512,512]{4,3,2,1,0:T(8,128)S(1)} %bitcast.14) | data formatting | bytes 4194304
Async XLA Ops:
  106.4 3.2 %copy-start = (f32[2,512,512]{2,1,0:T(8,128)S(1)}, f32[2,512,512]{2,1,0:T(8,128)}, u32[]{:S(2)}) copy-start(f32[2,512,512]{2,1,0:T(8,128)} %get-tuple-element.8) | copy-start | bytes 6291460

commit v2 on v0

v2 whole, which is shorter than its diff:
```python
import functools

import jax
import jax.numpy as jnp
from jax import lax
from jax.experimental import pallas as pl
from jax.experimental.pallas import tpu as pltpu
from jax.sharding import PartitionSpec as P

decay_keep = 0.9
epsilon = 1e-06
rms_limit = 0.5

MESH = pl.DeviceIdType.MESH
f32 = jnp.float32
bf16 = jnp.bfloat16

SIDE = 4
REPS = 16
COLS = 8
ROOT = 1
SLOTS = 2
BLOCK = 512
PIECE = 32
HALF = 16
WIDE = 128
STEPS = BLOCK // WIDE
BACK = 256
TURNS = BLOCK // BACK


def kernel(
    grads, owner_list, left_stat, right_stat, left_root, right_root,
    update, left_out, right_out,
    far_in, near_in, both_in, near_own, last_own,
    line_sum, line_far, line_near, line_both, line_in, piece,
    to_owner, block_in, root_in, root_hi, root_lo, stat_in, precond, ready,
    held_first, held_last, scale_own, scale_in, to_place,
    squares, squares_in, column, column_in, owners, table,
    load_sem, root_sem, stat_sem, list_sem,
    far_s, far_r, near_s, near_r, both_s, both_r,
    lfar_s, lfar_r, lnear_s, lnear_r, lboth_s, lboth_r, line_s, line_r,
    owner_s, owner_r, held_s, held_r, scale_s, scale_r, place_s, place_r,
    square_s, square_r, column_s, column_r,
):
    s = lax.axis_index("shard")
    r = lax.axis_index("replica")
    x, y = r % SIDE, r // SIDE
    held = (held_first, held_last)

    def along(half, step):
        if half == 0:
            return (s, y * SIDE + (x + step) % SIDE)
        return (s, (y + step) % SIDE * SIDE + x)

    def other(d):
        return (s, (r + d) % REPS)

    def send(src, dst, send_sem, recv_sem, device):
        return pltpu.make_async_remote_copy(
            src_ref=src, dst_ref=dst, send_sem=send_sem, recv_sem=recv_sem,
            device_id=device, device_id_type=MESH,
        )

    barrier = pltpu.get_barrier_semaphore()
    for half in range(2):
        for step in (1, 3):
            pl.semaphore_signal(barrier, inc=1, device_id=along(half, step), device_id_type=MESH)

    @pl.when(s == ROOT)
    def _():
        @pl.loop(1, COLS)
        def _(d):
            pl.semaphore_signal(barrier, inc=1, device_id=((s + d) % COLS, r), device_id_type=MESH)

        pl.semaphore_wait(barrier, 4)

    @pl.when(s != ROOT)
    def _():
        pl.semaphore_wait(barrier, 5)

    def chunk(g, step, first, count):
        wide, half = g // 2, g % 2
        place = ((x if half == 0 else y) + step) % SIDE
        rows = pl.ds(first, count)
        cols = pl.ds(wide * WIDE, WIDE)
        if half == 0:
            return grads.at[rows, :, place, 0, :, cols]
        return grads.at[rows, place, :, 1, :, cols]

    def far(g, way):
        return send(chunk(g, 2, 8 * way, 8), far_in.at[g, way],
                    far_s.at[g, way], far_r.at[g, way], along(g % 2, 1 - 2 * way))

    def near(g, way):
        return send(chunk(g, 1 - 2 * way, 8 - 8 * way, 8), near_in.at[g, way],
                    near_s.at[g, way], near_r.at[g, way], along(g % 2, 1 - 2 * way))

    def both(g, way):
        return send(near_own.at[g, way], both_in.at[g, way],
                    both_s.at[g, way], both_r.at[g, way], along(g % 2, 1 - 2 * way))

    def load_near(g, way):
        return pltpu.make_async_copy(chunk(g, 1 - 2 * way, 8 * way, 8),
                                     near_own.at[g, way], load_sem.at[g, way])

    def load_last(g):
        return pltpu.make_async_copy(chunk(g, 0, 0, REPS), last_own.at[g], load_sem.at[g, 2])

    def line_place(g, step):
        return ((y if g % 2 == 0 else x) + step) % SIDE

    def line(g, d):
        return send(line_sum.at[g, line_place(g, d)], line_in.at[g % 2, d - 1],
                    line_s.at[g % 2, d - 1], line_r.at[g % 2, d - 1], along(1 - g % 2, d))

    def lfar(g, way):
        return send(line_sum.at[g, line_place(g, 2), pl.ds(8 * way, 8)], line_far.at[g, way],
                    lfar_s.at[g, way], lfar_r.at[g, way], along(1 - g % 2, 1 - 2 * way))

    def lnear(g, way):
        return send(line_sum.at[g, line_place(g, 1 - 2 * way), pl.ds(8 - 8 * way, 8)],
                    line_near.at[g, way],
                    lnear_s.at[g, way], lnear_r.at[g, way], along(1 - g % 2, 1 - 2 * way))

    def lboth(g, way):
        return send(line_sum.at[g, line_place(g, 1 - 2 * way), pl.ds(8 * way, 8)],
                    line_both.at[g, way],
                    lboth_s.at[g, way], lboth_r.at[g, way], along(1 - g % 2, 1 - 2 * way))

    def direct(wide):
        return wide == STEPS - 1

    def start_far(wide):
        for g in (2 * wide, 2 * wide + 1):
            for way in range(2):
                far(g, way).start()
                load_near(g, way).start()

    def start_near(wide):
        for g in (2 * wide, 2 * wide + 1):
            for way in range(2):
                near(g, way).start()
            load_last(g).start()

    def combine(wide):
        for g in (2 * wide, 2 * wide + 1):
            for way in range(2):
                load_near(g, way).wait()
                far(g, way).wait_recv()

                @pl.loop(0, 8)
                def _(b):
                    near_own[g, way, b] = near_own[g, way, b] + far_in[g, way, b]

                both(g, way).start()

    def line_total(wide):
        for g in (2 * wide, 2 * wide + 1):
            load_last(g).wait()
            for way in range(2):
                near(g, way).wait_recv()
                both(g, way).wait_recv()

            @pl.loop(0, 8)
            def _(b):
                for way in range(2):
                    total = (last_own[g, 8 * way + b].astype(f32)
                             + both_in[g, way, b].astype(f32)
                             + near_in[g, 1 - way, b].astype(f32))
                    line_sum[g, :, 8 * way + b] = total.astype(bf16)

            if direct(wide):
                for d in (2, 1, 3):
                    line(g, d).start()
            else:
                for way in range(2):
                    lfar(g, way).start()
                for way in range(2):
                    lnear(g, way).start()

    def line_combine(wide):
        if direct(wide):
            return
        for g in (2 * wide, 2 * wide + 1):
            for way in range(2):
                lfar(g, way).wait_recv()
                place = line_place(g, 1 - 2 * way)

                @pl.loop(0, 8)
                def _(b):
                    line_sum[g, place, 8 * way + b] = (
                        line_sum[g, place, 8 * way + b] + line_far[g, way, b])

                lboth(g, way).start()

    def total(wide):
        for g in (2 * wide, 2 * wide + 1):
            place = line_place(g, 0)

            def finish(b, value):
                value = value.astype(bf16)
                piece[wide, b, pl.ds(g % 2 * HALF, HALF), :] = value
                value = value.astype(f32)
                value = value * value
                squares[...] += value[:8] + value[8:]

            if direct(wide):
                for d in (1, 2, 3):
                    line(g, d).wait_recv()

                @pl.loop(0, REPS)
                def _(b):
                    value = line_sum[g, place, b].astype(f32)
                    for d in range(3):
                        value = value + line_in[g % 2, d, b].astype(f32)
                    finish(b, value)
            else:
                for way in range(2):
                    lnear(g, way).wait_recv()
                    lboth(g, way).wait_recv()

                @pl.loop(0, 8)
                def _(b):
                    for way in range(2):
                        finish(8 * way + b,
                               line_sum[g, place, 8 * way + b].astype(f32)
                               + line_both[g, way, b].astype(f32)
                               + line_near[g, 1 - way, b].astype(f32))

    def columns(wide):
        return pl.ds(wide * WIDE, WIDE)

    def owner(wide, d):
        return send(to_owner.at[wide, (r + d) % REPS], block_in.at[:, r, :, columns(wide)],
                    owner_s.at[wide, d], owner_r.at[wide, d], other(d))

    def route(wide):
        @pl.loop(0, REPS)
        def _(o):
            for k in range(SLOTS):
                to_owner[wide, o, k] = piece[wide, table[0, o * SLOTS + k]]

        @pl.loop(1, REPS)
        def _(d):
            owner(wide, d).start()

        block_in[:, r, :, columns(wide)] = to_owner[wide, r]

    def wait_route(wide):
        @pl.loop(1, REPS)
        def _(d):
            owner(wide, d).wait_recv()

    roots = [pltpu.make_async_copy(ref, root_in.at[i], root_sem.at[i])
             for i, ref in enumerate((left_root, right_root))]
    stats = [pltpu.make_async_copy(ref, stat_in.at[i], stat_sem.at[i])
             for i, ref in enumerate((left_stat, right_stat))]

    names = pltpu.make_async_copy(owner_list, owners, list_sem)

    start_far(0)
    names.start()
    start_near(0)
    start_far(1)
    for copy in roots:
        copy.start()

    names.wait()

    @pl.loop(0, REPS)
    def _(j):
        mine = owners[0, s * REPS + j]
        count = jnp.int32(0)
        for i in range(REPS):
            hit = (owners[0, s * REPS + i] == mine) & (i < j)
            count = count + hit.astype(jnp.int32)
        table[1, j] = mine
        table[2, j] = jnp.minimum(count, SLOTS - 1)

    @pl.loop(0, REPS)
    def _(o):
        first, second = jnp.int32(REPS), jnp.int32(REPS)
        for j in range(REPS):
            hit = table[1, j] == o
            first = jnp.where(hit & (table[2, j] == 0), j, first)
            second = jnp.where(hit & (table[2, j] == 1), j, second)
        table[0, o * SLOTS] = first
        table[0, o * SLOTS + 1] = second

    for wide in range(STEPS):
        piece[wide, REPS] = jnp.zeros((PIECE, WIDE), bf16)
    squares[...] = jnp.zeros_like(squares)

    def split(side):
        roots[side].wait()

        @pl.loop(0, SLOTS * 8)
        def _(i):
            k, t = i // 8, i % 8
            rows = pl.ds(pl.multiple_of(t * 64, 64), 64)
            whole = root_in[side, k, rows, :]
            top = whole.astype(bf16)
            root_hi[side, k, rows, :] = top
            root_lo[side, k, rows, :] = (whole - top.astype(f32)).astype(bf16)

    for wide in range(STEPS):
        combine(wide)
        if wide + 1 < STEPS:
            start_near(wide + 1)
        if wide + 2 < STEPS:
            start_far(wide + 2)
        if wide < 2:
            split(wide)
        line_total(wide)
        if wide == 0:
            for copy in stats:
                copy.start()
        if wide >= 1:
            line_combine(wide - 1)
        if wide >= 2:
            total(wide - 2)
            route(wide - 2)
    line_combine(STEPS - 1)
    for wide in (STEPS - 2, STEPS - 1):
        total(wide)
        route(wide)

    def square(d):
        return send(squares, squares_in.at[d], square_s.at[d], square_r.at[d], other(d))

    @pl.loop(1, REPS)
    def _(d):
        square(d).start()

    def product(first, count):
        @pl.loop(0, SLOTS * 2)
        def _(i):
            t, k = i // 2, i % 2
            rows = pl.ds(pl.multiple_of(t * 256, 256), 256)
            across = pl.ds(first, count)
            block = block_in[k, :, :, across].reshape(BLOCK, count)
            part = (jnp.dot(root_hi[0, k, rows, :], block, preferred_element_type=f32)
                    + jnp.dot(root_lo[0, k, rows, :], block, preferred_element_type=f32))
            top = part.astype(bf16)
            low = (part - top.astype(f32)).astype(bf16)
            hi, lo = root_hi[1, k, across, :], root_lo[1, k, across, :]
            value = (jnp.dot(top, hi, preferred_element_type=f32)
                     + jnp.dot(top, lo, preferred_element_type=f32)
                     + jnp.dot(low, hi, preferred_element_type=f32))
            if first == 0:
                precond[k, rows, :] = value
            else:
                value = precond[k, rows, :] + value
                precond[k, rows, :] = value
            if first + count == BLOCK:
                ready[k, pl.ds(t * 8, 8)] = value.astype(bf16).reshape(8, PIECE, BLOCK)

    def gather_column(d, value):
        square(d).wait_recv()
        return value + squares_in[d]

    def column_send(to_root):
        if to_root is None:
            return send(column.at[0], column_in.at[s], column_s.at[0], column_r.at[s], (ROOT, r))
        place = (ROOT + to_root) % COLS
        return send(column.at[1], column_in.at[ROOT], column_s.at[to_root], column_r.at[ROOT], (place, r))

    def column_from(d):
        place = (ROOT + d) % COLS
        return send(column.at[0], column_in.at[place], column_s.at[0], column_r.at[place], (ROOT, r))

    wait_route(0)
    wait_route(1)
    product(0, 2 * WIDE)
    wait_route(2)
    product(2 * WIDE, WIDE)

    all_squares = lax.fori_loop(1, REPS, gather_column, squares[...])
    column[0] = jnp.sum(all_squares, axis=0, keepdims=True)

    @pl.when(s != ROOT)
    def _():
        column_send(None).start()

    wait_route(3)
    product(3 * WIDE, WIDE)

    def hold(turn, d):
        return send(ready.at[:, (r + d) % REPS, :, pl.ds(turn * BACK, BACK)], held[turn].at[r],
                    held_s.at[turn, d], held_r.at[turn, d], other(d))

    for turn in range(TURNS):
        @pl.loop(1, REPS)
        def _(d):
            hold(turn, d).start()

        held[turn][r] = ready[:, r, :, pl.ds(turn * BACK, BACK)]

    for k in range(SLOTS):
        def square_sum(i, carry):
            value, power = carry
            p = precond[k, pl.ds(pl.multiple_of(i * PIECE, PIECE), PIECE), :]
            g = block_in[k, i].astype(f32)
            return value + g * g, power + p * p

        zero = jnp.zeros((PIECE, BLOCK), f32)
        value, power = lax.fori_loop(0, REPS, square_sum, (zero, zero))
        value = jnp.sum(value, axis=(0, 1), keepdims=True) / (BLOCK * BLOCK)
        power = jnp.sum(power, axis=(0, 1), keepdims=True) / (BLOCK * BLOCK)
        scale = jnp.sqrt(value + epsilon) / jnp.sqrt(power + epsilon)
        scale_own[pl.ds(k, 1), :] = jnp.broadcast_to(scale, (1, 128))

    def scale_send(d):
        return send(scale_own, scale_in.at[r], scale_s.at[d], scale_r.at[d], other(d))

    @pl.loop(1, REPS)
    def _(d):
        scale_send(d).start()

    scale_in[r] = scale_own[...]

    @pl.when(s == ROOT)
    def _():
        def gather(d, value):
            column_from(d).wait_recv()
            return value + column_in[(ROOT + d) % COLS]

        column[1] = lax.fori_loop(1, COLS, gather, column[0])
        column_in[ROOT] = column[1]

        @pl.loop(1, COLS)
        def _(d):
            column_send(d).start()

    for copy in stats:
        copy.wait()

    @pl.loop(0, SLOTS)
    def _(k):
        filled = table[0, r * SLOTS + k] < REPS
        keep = jnp.where(filled, decay_keep, 1.0).astype(f32)
        weight = (1.0 - decay_keep) / BLOCK
        for t in range(2):
            rows = pl.ds(t * 256, 256)
            block = block_in[k].reshape(BLOCK, BLOCK)
            left = lax.dot_general(
                block[t * 256:(t + 1) * 256], block, (((1,), (1,)), ((), ())),
                preferred_element_type=f32)
            left_out[k, rows, :] = keep * stat_in[0, k, rows, :] + weight * left
            right = lax.dot_general(
                block[:, t * 256:(t + 1) * 256], block, (((0,), (0,)), ((), ())),
                preferred_element_type=f32)
            right_out[k, rows, :] = keep * stat_in[1, k, rows, :] + weight * right

    @pl.when(s != ROOT)
    def _():
        send(column.at[1], column_in.at[ROOT], column_s.at[1], column_r.at[ROOT], (ROOT, r)).wait_recv()

    rms = jnp.sqrt(jnp.sum(column_in[ROOT], axis=(0, 1), keepdims=True)
                   / (COLS * REPS * BLOCK * BLOCK))
    clip = jnp.minimum(1.0, rms_limit / rms)

    @pl.loop(1, REPS)
    def _(d):
        scale_send(d).wait_recv()

    def settle(turn, d):
        return send(to_place.at[turn, (r + d) % REPS], update.at[r, :, pl.ds(turn * BACK, BACK)],
                    place_s.at[turn, d], place_r.at[turn, d], other(d))

    for turn in range(TURNS):
        @pl.loop(1, REPS)
        def _(d):
            hold(turn, d).wait_recv()

        @pl.loop(0, REPS)
        def _(j):
            o, k = table[1, j], table[2, j]
            both_scales = scale_in[o]
            scale = jnp.where(k == 0, both_scales[:1], both_scales[1:]) * clip
            value = held[turn][o, k].astype(f32)
            for part in range(BACK // 128):
                to_place[turn, j, :, pl.ds(part * 128, 128)] = (
                    value[:, part * 128:(part + 1) * 128] * scale).astype(bf16)

        @pl.loop(1, REPS)
        def _(d):
            settle(turn, d).start()

        update[r, :, pl.ds(turn * BACK, BACK)] = to_place[turn, r]

    for g in range(2 * STEPS):
        for way in range(2):
            far(g, way).wait_send()
            near(g, way).wait_send()
            both(g, way).wait_send()
            if not direct(g // 2):
                lfar(g, way).wait_send()
                lnear(g, way).wait_send()
                lboth(g, way).wait_send()
        if direct(g // 2):
            for d in (1, 2, 3):
                line(g, d).wait_send()

    @pl.when(s != ROOT)
    def _():
        column_send(None).wait_send()

    @pl.when(s == ROOT)
    def _():
        @pl.loop(1, COLS)
        def _(d):
            column_send(d).wait_send()

    @pl.loop(1, REPS)
    def _(d):
        square(d).wait_send()
        scale_send(d).wait_send()
        for wide in range(STEPS):
            owner(wide, d).wait_send()
        for turn in range(TURNS):
            hold(turn, d).wait_send()
            settle(turn, d).wait_send()
            settle(turn, d).wait_recv()


def on_device(partial_grads, owner_list, left_stat, right_stat, left_root, right_root):
    grads = partial_grads.reshape(REPS, SIDE, SIDE, 2, HALF, BLOCK)
    hbm_spec = pl.BlockSpec(memory_space=pltpu.HBM)
    vmem_spec = pl.BlockSpec(memory_space=pltpu.VMEM)
    dma = pltpu.SemaphoreType.DMA
    groups = 2 * STEPS
    quarter = pltpu.VMEM((groups, 2, 8, SIDE, HALF, WIDE), bf16)
    eighth = pltpu.VMEM((groups, 2, 8, HALF, WIDE), bf16)
    pair = [dma((groups, 2))] * 2
    state = pltpu.VMEM((SLOTS, BLOCK, BLOCK), f32)
    update, left_new, right_new = pl.pallas_call(
        kernel,
        out_shape=(pltpu.VMEM((REPS, PIECE, BLOCK), bf16), state, state),
        in_specs=[hbm_spec] * 6,
        out_specs=(vmem_spec, vmem_spec, vmem_spec),
        scratch_shapes=[
            quarter, quarter, quarter, quarter,
            pltpu.VMEM((groups, REPS, SIDE, HALF, WIDE), bf16),
            pltpu.VMEM((groups, SIDE, REPS, HALF, WIDE), bf16),
            eighth, eighth, eighth,
            pltpu.VMEM((2, 3, REPS, HALF, WIDE), bf16),
            pltpu.VMEM((STEPS, REPS + 1, PIECE, WIDE), bf16),
            pltpu.VMEM((STEPS, REPS, SLOTS, PIECE, WIDE), bf16),
            pltpu.VMEM((SLOTS, REPS, PIECE, BLOCK), bf16),
            pltpu.VMEM((2, SLOTS, BLOCK, BLOCK), f32),
            pltpu.VMEM((2, SLOTS, BLOCK, BLOCK), bf16),
            pltpu.VMEM((2, SLOTS, BLOCK, BLOCK), bf16),
            pltpu.VMEM((2, SLOTS, BLOCK, BLOCK), f32),
            pltpu.VMEM((SLOTS, BLOCK, BLOCK), f32),
            pltpu.VMEM((SLOTS, REPS, PIECE, BLOCK), bf16),
            pltpu.VMEM((REPS, SLOTS, PIECE, BACK), bf16),
            pltpu.VMEM((REPS, SLOTS, PIECE, BACK), bf16),
            pltpu.VMEM((SLOTS, 128), f32),
            pltpu.VMEM((REPS, SLOTS, 128), f32),
            pltpu.VMEM((TURNS, REPS, PIECE, BACK), bf16),
            pltpu.VMEM((8, 128), f32),
            pltpu.VMEM((REPS, 8, 128), f32),
            pltpu.VMEM((2, 1, 128), f32),
            pltpu.VMEM((COLS, 1, 128), f32),
            pltpu.SMEM((1, COLS * REPS), jnp.int32),
            pltpu.SMEM((3, REPS * SLOTS), jnp.int32),
            dma((groups, 3)), dma((2,)), dma((2,)), dma,
        ] + pair * 6 + [dma((2, 3))] * 2 + [dma((STEPS, REPS))] * 2
        + [dma((TURNS, REPS))] * 2 + [dma((REPS,))] * 2 + [dma((TURNS, REPS))] * 2
        + [dma((REPS,))] * 2 + [dma((COLS,))] * 2,
        compiler_params=pltpu.CompilerParams(
            collective_id=0, has_side_effects=True, vmem_limit_bytes=58 << 20),
    )(grads, owner_list.reshape(1, COLS * REPS),
      left_stat[0, 0], right_stat[0, 0], left_root[0, 0], right_root[0, 0])
    return (update.reshape(1, BLOCK, BLOCK), left_new[None, None], right_new[None, None])


def solution(mesh):
    return jax.shard_map(
        on_device,
        mesh=mesh,
        in_specs=(
            P("replica", "shard", None, None),
            P(),
            P("shard", "replica", None, None, None),
            P("shard", "replica", None, None, None),
            P("shard", "replica", None, None, None),
            P("shard", "replica", None, None, None),
        ),
        out_specs=(
            P(("shard", "replica"), None, None),
            P("shard", "replica", None, None, None),
            P("shard", "replica", None, None, None),
        ),
        check_vma=False,
    )
```

time: 393 us -> 97.1 us (0.25)
  waiting for transfers between devices: 263 us -> 0 us
  Pallas kernels: 0 us -> 92.9 us
  blocking collectives: 64.9 us -> 0 us
  matrix products: 40.7 us -> 0 us
  between operations: 15.8 us -> 0.64 us
  other arithmetic: 3.93 us -> 0 us
    all_gather x2 -> x0, waiting for transfers between devices: 171 us -> none  [the longest x1 99.2 us: on_device(): block_piece = lax.all_gather(ready, 'replica', axis=0, tiled=True)]
    pallas_call x0 -> x1, Pallas kernels: none -> 92.9 us  [on_device(): pl.pallas_call(kernel, out_shape=(pltpu.VMEM((REPS, PIECE, BLOCK), bf16),...]
    unnamed x4 -> x0, waiting for transfers between devices: 91.8 us -> none
    psum x1 -> x0, blocking collectives: 64.9 us -> none  [on_device(): total_sq = lax.psum(jnp.sum(grad_wide * grad_wide), ('shard', 'replica'))]
    dot_general x6 -> x0, matrix products: 40.7 us -> none  [the longest x1 15.5 us: on_device(): jnp.einsum('p,pab->ab', weight, block_piece, preferred_element_type=jnp.f...]
  transfers between devices with their start and end apart: 3 -> 0, of which waited for: 3 -> 0; matrix products, arithmetic and copies ran while one was open for 2% -> 0% of each run, Pallas kernels for 0% -> 0%
where the time goes in v2:
time: 97.1 us; the launch traced here: 97 us
  Pallas kernels  92.9 us (96%)
  local copies, waits for them, and re-layouts  3.43 us (4%)
    pallas_call x1, Pallas kernels, on_device(): pl.pallas_call(kernel, out_shape=(pltpu.VMEM((REPS, PIECE, BLOCK), bf16),...  92.9 us
    unnamed x3, local copies, waits for them, and re-layouts  3.43 us

profile of v2, /device:TPU:0, one launch (start us, length us, event | category | flops | bytes accessed | tf_op | source)
XLA Modules:
  0.0 97.0 jit_solution(3042042393004734810)
XLA Ops:
  0.6 92.9 %shard_map.85 = (bf16[16,32,512]{2,1,0:T(8,128)(2,1)S(1)}, f32[2,512,512]{2,1,0:T(8,128)S(1)}, f32[2,512,512]{2,1,0:T(8,128)S(1)}) custom-call(bf16[16,4,4,2,16,512]{5,4,3,2,1,0:T(8,128)(2,1)} %bitcast.12, s32[1,128]{1,0:T(1,128)} %bitcast.17, f32[2,512,512]{2,1,0:T(8,128)} %bitcast.13, f32[2,512,512]{2,1,0:T(8,128)} %bitcast.14, f32[2,512,512]{2,1,0:T(8,128)} %bitcast.15, ...), custom_call_target="tpu_custom_call" | custom-call | tf_op jit(solution)/shard_map/pallas_call | solution.py:538
  93.6 0.8 copy.12
  94.4 1.3 %copy.13 = f32[1,1,2,512,512]{4,3,2,1,0:T(8,128)} copy(f32[1,1,2,512,512]{4,3,2,1,0:T(8,128)S(1)} %bitcast.10) | data formatting | bytes 4194304
  95.7 1.3 %copy.14 = f32[1,1,2,512,512]{4,3,2,1,0:T(8,128)} copy(f32[1,1,2,512,512]{4,3,2,1,0:T(8,128)S(1)} %bitcast.9) | data formatting | bytes 4194304

commit v3 on v2

--- a/solution.py
+++ b/solution.py
@@ -32,15 +32,14 @@
 def kernel(
     grads, owner_list, left_stat, right_stat, left_root, right_root,
     update, left_out, right_out,
-    far_in, near_in, both_in, near_own, last_own,
-    line_sum, line_far, line_near, line_both, line_in, piece,
+    far_in, pass_in, near_own, last_own,
+    line_sum, line_far, line_pass, line_in, piece,
     to_owner, block_in, root_in, root_hi, root_lo, stat_in, precond, ready,
     held_first, held_last, scale_own, scale_in, to_place,
     squares, squares_in, column, column_in, owners, table,
-    load_sem, root_sem, stat_sem, list_sem,
-    far_s, far_r, near_s, near_r, both_s, both_r,
-    lfar_s, lfar_r, lnear_s, lnear_r, lboth_s, lboth_r, line_s, line_r,
-    owner_s, owner_r, held_s, held_r, scale_s, scale_r, place_s, place_r,
+    near_sem, last_sem, root_sem, stat_sem, list_sem,
+    far_s, far_r, near_s, both_s, pass_r, lfar_s, lfar_r, lnear_s, lboth_s, lpass_r,
+    line_s, line_r, owner_s, owner_r, held_s, held_r, scale_s, scale_r, place_s, place_r,
     square_s, square_r, column_s, column_r,
 ):
     s = lax.axis_index("shard")
@@ -61,6 +60,15 @@
             src_ref=src, dst_ref=dst, send_sem=send_sem, recv_sem=recv_sem,
             device_id=device, device_id_type=MESH,
         )
+
+    def landed(ref, sem):
+        send(ref, ref, column_s, sem, other(1)).wait_recv()
+
+    def left(ref, sem):
+        send(ref, ref, sem, column_r, other(1)).wait_send()
+
+    def loaded(ref, sem):
+        pltpu.make_async_copy(ref, ref, sem).wait()
 
     barrier = pltpu.get_barrier_semaphore()
     for half in range(2):
@@ -90,43 +98,46 @@
 
     def far(g, way):
         return send(chunk(g, 2, 8 * way, 8), far_in.at[g, way],
-                    far_s.at[g, way], far_r.at[g, way], along(g % 2, 1 - 2 * way))
+                    far_s, far_r.at[g // 2], along(g % 2, 1 - 2 * way))
 
     def near(g, way):
-        return send(chunk(g, 1 - 2 * way, 8 - 8 * way, 8), near_in.at[g, way],
-                    near_s.at[g, way], near_r.at[g, way], along(g % 2, 1 - 2 * way))
+        return send(chunk(g, 1 - 2 * way, 8 - 8 * way, 8), pass_in.at[g, 0, way],
+                    near_s, pass_r.at[g // 2], along(g % 2, 1 - 2 * way))
 
     def both(g, way):
-        return send(near_own.at[g, way], both_in.at[g, way],
-                    both_s.at[g, way], both_r.at[g, way], along(g % 2, 1 - 2 * way))
+        return send(near_own.at[g, way], pass_in.at[g, 1, way],
+                    both_s, pass_r.at[g // 2], along(g % 2, 1 - 2 * way))
 
     def load_near(g, way):
         return pltpu.make_async_copy(chunk(g, 1 - 2 * way, 8 * way, 8),
-                                     near_own.at[g, way], load_sem.at[g, way])
+                                     near_own.at[g, way], near_sem.at[g // 2])
 
     def load_last(g):
-        return pltpu.make_async_copy(chunk(g, 0, 0, REPS), last_own.at[g], load_sem.at[g, 2])
+        return pltpu.make_async_copy(chunk(g, 0, 0, REPS), last_own.at[g], last_sem.at[g // 2])
 
     def line_place(g, step):
         return ((y if g % 2 == 0 else x) + step) % SIDE
 
     def line(g, d):
         return send(line_sum.at[g, line_place(g, d)], line_in.at[g % 2, d - 1],
-                    line_s.at[g % 2, d - 1], line_r.at[g % 2, d - 1], along(1 - g % 2, d))
+                    line_s, line_r, along(1 - g % 2, d))
 
     def lfar(g, way):
         return send(line_sum.at[g, line_place(g, 2), pl.ds(8 * way, 8)], line_far.at[g, way],
-                    lfar_s.at[g, way], lfar_r.at[g, way], along(1 - g % 2, 1 - 2 * way))
+                    lfar_s, lfar_r.at[g // 2], along(1 - g % 2, 1 - 2 * way))
 
     def lnear(g, way):
         return send(line_sum.at[g, line_place(g, 1 - 2 * way), pl.ds(8 - 8 * way, 8)],
-                    line_near.at[g, way],
-                    lnear_s.at[g, way], lnear_r.at[g, way], along(1 - g % 2, 1 - 2 * way))
+                    line_pass.at[g, 0, way],
+                    lnear_s, lpass_r.at[g // 2], along(1 - g % 2, 1 - 2 * way))
 
     def lboth(g, way):
         return send(line_sum.at[g, line_place(g, 1 - 2 * way), pl.ds(8 * way, 8)],
-                    line_both.at[g, way],
-                    lboth_s.at[g, way], lboth_r.at[g, way], along(1 - g % 2, 1 - 2 * way))
+                    line_pass.at[g, 1, way],
+                    lboth_s, lpass_r.at[g // 2], along(1 - g % 2, 1 - 2 * way))
+
+    def pair(wide):
+        return pl.ds(2 * wide, 2)
 
     def direct(wide):
         return wide == STEPS - 1
@@ -144,11 +155,10 @@
             load_last(g).start()
 
     def combine(wide):
+        loaded(near_own.at[pair(wide)], near_sem.at[wide])
+        landed(far_in.at[pair(wide)], far_r.at[wide])
         for g in (2 * wide, 2 * wide + 1):
             for way in range(2):
-                load_near(g, way).wait()
-                far(g, way).wait_recv()
-
                 @pl.loop(0, 8)
                 def _(b):
                     near_own[g, way, b] = near_own[g, way, b] + far_in[g, way, b]
@@ -156,18 +166,15 @@
                 both(g, way).start()
 
     def line_total(wide):
+        loaded(last_own.at[pair(wide)], last_sem.at[wide])
+        landed(pass_in.at[pair(wide)], pass_r.at[wide])
         for g in (2 * wide, 2 * wide + 1):
-            load_last(g).wait()
-            for way in range(2):
-                near(g, way).wait_recv()
-                both(g, way).wait_recv()
-
             @pl.loop(0, 8)
             def _(b):
                 for way in range(2):
                     total = (last_own[g, 8 * way + b].astype(f32)
-                             + both_in[g, way, b].astype(f32)
-                             + near_in[g, 1 - way, b].astype(f32))
+                             + pass_in[g, 1, way, b].astype(f32)
+                             + pass_in[g, 0, 1 - way, b].astype(f32))
                     line_sum[g, :, 8 * way + b] = total.astype(bf16)
 
             if direct(wide):
@@ -180,11 +187,9 @@
                     lnear(g, way).start()
 
     def line_combine(wide):
-        if direct(wide):
-            return
+        landed(line_far.at[pair(wide)], lfar_r.at[wide])
         for g in (2 * wide, 2 * wide + 1):
             for way in range(2):
-                lfar(g, way).wait_recv()
                 place = line_place(g, 1 - 2 * way)
 
                 @pl.loop(0, 8)
@@ -195,6 +200,10 @@
                 lboth(g, way).start()
 
     def total(wide):
+        if direct(wide):
+            landed(line_in, line_r)
+        else:
+            landed(line_pass.at[pair(wide)], lpass_r.at[wide])
         for g in (2 * wide, 2 * wide + 1):
             place = line_place(g, 0)
 
@@ -206,9 +215,6 @@
                 squares[...] += value[:8] + value[8:]
 
             if direct(wide):
-                for d in (1, 2, 3):
-                    line(g, d).wait_recv()
-
                 @pl.loop(0, REPS)
                 def _(b):
                     value = line_sum[g, place, b].astype(f32)
@@ -216,24 +222,20 @@
                         value = value + line_in[g % 2, d, b].astype(f32)
                     finish(b, value)
             else:
-                for way in range(2):
-                    lnear(g, way).wait_recv()
-                    lboth(g, way).wait_recv()
-
                 @pl.loop(0, 8)
                 def _(b):
                     for way in range(2):
                         finish(8 * way + b,
                                line_sum[g, place, 8 * way + b].astype(f32)
-                               + line_both[g, way, b].astype(f32)
-                               + line_near[g, 1 - way, b].astype(f32))
+                               + line_pass[g, 1, way, b].astype(f32)
+                               + line_pass[g, 0, 1 - way, b].astype(f32))
 
     def columns(wide):
         return pl.ds(wide * WIDE, WIDE)
 
     def owner(wide, d):
         return send(to_owner.at[wide, (r + d) % REPS], block_in.at[:, r, :, columns(wide)],
-                    owner_s.at[wide, d], owner_r.at[wide, d], other(d))
+                    owner_s, owner_r.at[wide], other(d))
 
     def route(wide):
         @pl.loop(0, REPS)
@@ -248,9 +250,7 @@
         block_in[:, r, :, columns(wide)] = to_owner[wide, r]
 
     def wait_route(wide):
-        @pl.loop(1, REPS)
-        def _(d):
-            owner(wide, d).wait_recv()
+        landed(block_in.at[:, pl.ds(0, REPS - 1), :, columns(wide)], owner_r.at[wide])
 
     roots = [pltpu.make_async_copy(ref, root_in.at[i], root_sem.at[i])
              for i, ref in enumerate((left_root, right_root))]
@@ -312,22 +312,20 @@
             start_far(wide + 2)
         if wide < 2:
             split(wide)
+        if wide >= 1:
+            line_combine(wide - 1)
         line_total(wide)
         if wide == 0:
             for copy in stats:
                 copy.start()
         if wide >= 1:
-            line_combine(wide - 1)
-        if wide >= 2:
-            total(wide - 2)
-            route(wide - 2)
-    line_combine(STEPS - 1)
-    for wide in (STEPS - 2, STEPS - 1):
-        total(wide)
-        route(wide)
+            total(wide - 1)
+            route(wide - 1)
+    total(STEPS - 1)
+    route(STEPS - 1)
 
     def square(d):
-        return send(squares, squares_in.at[d], square_s.at[d], square_r.at[d], other(d))
+        return send(squares, squares_in.at[d], square_s, square_r, other(d))
 
     @pl.loop(1, REPS)
     def _(d):
@@ -357,18 +355,13 @@
                 ready[k, pl.ds(t * 8, 8)] = value.astype(bf16).reshape(8, PIECE, BLOCK)
 
     def gather_column(d, value):
-        square(d).wait_recv()
         return value + squares_in[d]
 
-    def column_send(to_root):
-        if to_root is None:
-            return send(column.at[0], column_in.at[s], column_s.at[0], column_r.at[s], (ROOT, r))
-        place = (ROOT + to_root) % COLS
-        return send(column.at[1], column_in.at[ROOT], column_s.at[to_root], column_r.at[ROOT], (place, r))
-
-    def column_from(d):
-        place = (ROOT + d) % COLS
-        return send(column.at[0], column_in.at[place], column_s.at[0], column_r.at[place], (ROOT, r))
+    def column_in_root():
+        return send(column.at[0], column_in.at[s], column_s, column_r, (ROOT, r))
+
+    def column_out(d):
+        return send(column.at[1], column_in.at[ROOT], column_s, column_r, ((ROOT + d) % COLS, r))
 
     wait_route(0)
     wait_route(1)
@@ -376,19 +369,20 @@
     wait_route(2)
     product(2 * WIDE, WIDE)
 
+    landed(squares_in.at[pl.ds(1, REPS - 1)], square_r)
     all_squares = lax.fori_loop(1, REPS, gather_column, squares[...])
     column[0] = jnp.sum(all_squares, axis=0, keepdims=True)
 
     @pl.when(s != ROOT)
     def _():
-        column_send(None).start()
+        column_in_root().start()
 
     wait_route(3)
     product(3 * WIDE, WIDE)
 
     def hold(turn, d):
         return send(ready.at[:, (r + d) % REPS, :, pl.ds(turn * BACK, BACK)], held[turn].at[r],
-                    held_s.at[turn, d], held_r.at[turn, d], other(d))
+                    held_s, held_r.at[turn], other(d))
 
     for turn in range(TURNS):
         @pl.loop(1, REPS)
@@ -412,7 +406,7 @@
         scale_own[pl.ds(k, 1), :] = jnp.broadcast_to(scale, (1, 128))
 
     def scale_send(d):
-        return send(scale_own, scale_in.at[r], scale_s.at[d], scale_r.at[d], other(d))
+        return send(scale_own, scale_in.at[r], scale_s, scale_r, other(d))
 
     @pl.loop(1, REPS)
     def _(d):
@@ -422,8 +416,9 @@
 
     @pl.when(s == ROOT)
     def _():
+        landed(column_in.at[pl.ds(0, COLS - 1)], column_r)
+
         def gather(d, value):
-            column_from(d).wait_recv()
             return value + column_in[(ROOT + d) % COLS]
 
         column[1] = lax.fori_loop(1, COLS, gather, column[0])
@@ -431,7 +426,7 @@
 
         @pl.loop(1, COLS)
         def _(d):
-            column_send(d).start()
+            column_out(d).start()
 
     for copy in stats:
         copy.wait()
@@ -455,24 +450,20 @@
 
     @pl.when(s != ROOT)
     def _():
-        send(column.at[1], column_in.at[ROOT], column_s.at[1], column_r.at[ROOT], (ROOT, r)).wait_recv()
+        landed(column_in.at[ROOT], column_r)
 
     rms = jnp.sqrt(jnp.sum(column_in[ROOT], axis=(0, 1), keepdims=True)
                    / (COLS * REPS * BLOCK * BLOCK))
     clip = jnp.minimum(1.0, rms_limit / rms)
 
-    @pl.loop(1, REPS)
-    def _(d):
-        scale_send(d).wait_recv()
+    landed(scale_in.at[pl.ds(0, REPS - 1)], scale_r)
 
     def settle(turn, d):
         return send(to_place.at[turn, (r + d) % REPS], update.at[r, :, pl.ds(turn * BACK, BACK)],
-                    place_s.at[turn, d], place_r.at[turn, d], other(d))
+                    place_s, place_r, other(d))
 
     for turn in range(TURNS):
-        @pl.loop(1, REPS)
-        def _(d):
-            hold(turn, d).wait_recv()
+        landed(held[turn].at[pl.ds(0, REPS - 1)], held_r.at[turn])
 
         @pl.loop(0, REPS)
         def _(j):
@@ -490,39 +481,28 @@
 
         update[r, :, pl.ds(turn * BACK, BACK)] = to_place[turn, r]
 
-    for g in range(2 * STEPS):
-        for way in range(2):
-            far(g, way).wait_send()
-            near(g, way).wait_send()
-            both(g, way).wait_send()
-            if not direct(g // 2):
-                lfar(g, way).wait_send()
-                lnear(g, way).wait_send()
-                lboth(g, way).wait_send()
-        if direct(g // 2):
-            for d in (1, 2, 3):
-                line(g, d).wait_send()
+    left(far_in, far_s)
+    left(near_own, near_s)
+    left(near_own, both_s)
+    left(line_far, lfar_s)
+    left(line_far, lnear_s)
+    left(line_far, lboth_s)
+    left(line_in, line_s)
+    left(to_owner.at[:, pl.ds(0, REPS - 1)], owner_s)
+    left(ready.at[:, pl.ds(0, REPS - 1)], held_s)
+    left(to_place.at[:, pl.ds(0, REPS - 1)], place_s)
+    left(squares_in.at[pl.ds(1, REPS - 1)], square_s)
+    left(scale_in.at[pl.ds(0, REPS - 1)], scale_s)
 
     @pl.when(s != ROOT)
     def _():
-        column_send(None).wait_send()
+        left(column_in.at[ROOT], column_s)
 
     @pl.when(s == ROOT)
     def _():
-        @pl.loop(1, COLS)
-        def _(d):
-            column_send(d).wait_send()
-
-    @pl.loop(1, REPS)
-    def _(d):
-        square(d).wait_send()
-        scale_send(d).wait_send()
-        for wide in range(STEPS):
-            owner(wide, d).wait_send()
-        for turn in range(TURNS):
-            hold(turn, d).wait_send()
-            settle(turn, d).wait_send()
-            settle(turn, d).wait_recv()
+        left(column_in.at[pl.ds(0, COLS - 1)], column_s)
+
+    landed(update.at[pl.ds(0, REPS - 1)], place_r)
 
 
 def on_device(partial_grads, owner_list, left_stat, right_stat, left_root, right_root):
@@ -531,9 +511,9 @@
     vmem_spec = pl.BlockSpec(memory_space=pltpu.VMEM)
     dma = pltpu.SemaphoreType.DMA
     groups = 2 * STEPS
-    quarter = pltpu.VMEM((groups, 2, 8, SIDE, HALF, WIDE), bf16)
-    eighth = pltpu.VMEM((groups, 2, 8, HALF, WIDE), bf16)
-    pair = [dma((groups, 2))] * 2
+    lines = groups - 2
+    quarter = (2, 8, SIDE, HALF, WIDE)
+    eighth = (2, 8, HALF, WIDE)
     state = pltpu.VMEM((SLOTS, BLOCK, BLOCK), f32)
     update, left_new, right_new = pl.pallas_call(
         kernel,
@@ -541,10 +521,13 @@
         in_specs=[hbm_spec] * 6,
         out_specs=(vmem_spec, vmem_spec, vmem_spec),
         scratch_shapes=[
-            quarter, quarter, quarter, quarter,
+            pltpu.VMEM((groups,) + quarter, bf16),
+            pltpu.VMEM((groups, 2) + quarter, bf16),
+            pltpu.VMEM((groups,) + quarter, bf16),
             pltpu.VMEM((groups, REPS, SIDE, HALF, WIDE), bf16),
             pltpu.VMEM((groups, SIDE, REPS, HALF, WIDE), bf16),
-            eighth, eighth, eighth,
+            pltpu.VMEM((lines,) + eighth, bf16),
+            pltpu.VMEM((lines, 2) + eighth, bf16),
             pltpu.VMEM((2, 3, REPS, HALF, WIDE), bf16),
             pltpu.VMEM((STEPS, REPS + 1, PIECE, WIDE), bf16),
             pltpu.VMEM((STEPS, REPS, SLOTS, PIECE, WIDE), bf16),
@@ -566,10 +549,13 @@
             pltpu.VMEM((COLS, 1, 128), f32),
             pltpu.SMEM((1, COLS * REPS), jnp.int32),
             pltpu.SMEM((3, REPS * SLOTS), jnp.int32),
-            dma((groups, 3)), dma((2,)), dma((2,)), dma,
-        ] + pair * 6 + [dma((2, 3))] * 2 + [dma((STEPS, REPS))] * 2
-        + [dma((TURNS, REPS))] * 2 + [dma((REPS,))] * 2 + [dma((TURNS, REPS))] * 2
-        + [dma((REPS,))] * 2 + [dma((COLS,))] * 2,
+            dma((STEPS,)), dma((STEPS,)), dma((2,)), dma((2,)), dma,
+            dma, dma((STEPS,)), dma, dma, dma((STEPS,)),
+            dma, dma((STEPS - 1,)), dma, dma, dma((STEPS - 1,)),
+            dma, dma, dma, dma((STEPS,)),
+            dma, dma((TURNS,)), dma, dma, dma, dma,
+            dma, dma, dma, dma,
+        ],
         compiler_params=pltpu.CompilerParams(
             collective_id=0, has_side_effects=True, vmem_limit_bytes=58 << 20),
     )(grads, owner_list.reshape(1, COLS * REPS),

time: 97.1 us -> 93.1 us (0.959)
  Pallas kernels: 92.9 us -> 88.9 us
    pallas_call x1, Pallas kernels: 92.9 us -> 88.9 us  [on_device(): pl.pallas_call(kernel, out_shape=(pltpu.VMEM((REPS, PIECE, BLOCK), bf16),...]
where the time goes in v3:
time: 93.1 us; the launch traced here: 92.9 us
  Pallas kernels  88.9 us (95%)
  local copies, waits for them, and re-layouts  3.43 us (4%)
    pallas_call x1, Pallas kernels, on_device(): pl.pallas_call(kernel, out_shape=(pltpu.VMEM((REPS, PIECE, BLOCK), bf16),...  88.9 us
    unnamed x3, local copies, waits for them, and re-layouts  3.43 us

profile of v3, /device:TPU:0, one launch (start us, length us, event | category | flops | bytes accessed | tf_op | source)
XLA Modules:
  0.0 92.9 jit_solution(14542950240448812955)
XLA Ops:
  0.6 88.9 %shard_map.85 = (bf16[16,32,512]{2,1,0:T(8,128)(2,1)S(1)}, f32[2,512,512]{2,1,0:T(8,128)S(1)}, f32[2,512,512]{2,1,0:T(8,128)S(1)}) custom-call(bf16[16,4,4,2,16,512]{5,4,3,2,1,0:T(8,128)(2,1)} %bitcast.12, s32[1,128]{1,0:T(1,128)} %bitcast.17, f32[2,512,512]{2,1,0:T(8,128)} %bitcast.13, f32[2,512,512]{2,1,0:T(8,128)} %bitcast.14, f32[2,512,512]{2,1,0:T(8,128)} %bitcast.15, ...), custom_call_target="tpu_custom_call" | custom-call | tf_op jit(solution)/shard_map/pallas_call | solution.py:518
  89.5 0.8 copy.12
  90.3 1.3 %copy.13 = f32[1,1,2,512,512]{4,3,2,1,0:T(8,128)} copy(f32[1,1,2,512,512]{4,3,2,1,0:T(8,128)S(1)} %bitcast.10) | data formatting | bytes 4194304
  91.6 1.3 %copy.14 = f32[1,1,2,512,512]{4,3,2,1,0:T(8,128)} copy(f32[1,1,2,512,512]{4,3,2,1,0:T(8,128)S(1)} %bitcast.9) | data formatting | bytes 4194304

commit v4 on v3

--- a/solution.py
+++ b/solution.py
@@ -34,8 +34,8 @@
     update, left_out, right_out,
     far_in, pass_in, near_own, last_own,
     line_sum, line_far, line_pass, line_in, piece,
-    to_owner, block_in, root_in, root_hi, root_lo, stat_in, precond, ready,
-    held_first, held_last, scale_own, scale_in, to_place,
+    to_first, to_second, block_in, root_in, root_hi, root_lo, stat_in, precond, ready,
+    held_first, held_0, held_1, scale_own, scale_in, to_place,
     squares, squares_in, column, column_in, owners, table,
     near_sem, last_sem, root_sem, stat_sem, list_sem,
     far_s, far_r, near_s, both_s, pass_r, lfar_s, lfar_r, lnear_s, lboth_s, lpass_r,
@@ -45,15 +45,18 @@
     s = lax.axis_index("shard")
     r = lax.axis_index("replica")
     x, y = r % SIDE, r // SIDE
-    held = (held_first, held_last)
+    held = (held_0, held_1)
 
     def along(half, step):
         if half == 0:
             return (s, y * SIDE + (x + step) % SIDE)
         return (s, (y + step) % SIDE * SIDE + x)
 
+    def peer(d):
+        return (r + d) % REPS
+
     def other(d):
-        return (s, (r + d) % REPS)
+        return (s, peer(d))
 
     def send(src, dst, send_sem, recv_sem, device):
         return pltpu.make_async_remote_copy(
@@ -233,24 +236,46 @@
     def columns(wide):
         return pl.ds(wide * WIDE, WIDE)
 
-    def owner(wide, d):
-        return send(to_owner.at[wide, (r + d) % REPS], block_in.at[:, r, :, columns(wide)],
-                    owner_s, owner_r.at[wide], other(d))
-
-    def route(wide):
+    def owner_first(wide, d):
+        return send(to_first.at[wide, peer(d)], block_in.at[0, r, :, columns(wide)],
+                    owner_s.at[0], owner_r.at[wide], other(d))
+
+    def owner_second(turn, d):
+        return send(to_second.at[turn, peer(d)], block_in.at[1, r, :, pl.ds(turn * BACK, BACK)],
+                    owner_s.at[1], owner_r.at[STEPS + turn], other(d))
+
+    def route_first(wide):
         @pl.loop(0, REPS)
         def _(o):
-            for k in range(SLOTS):
-                to_owner[wide, o, k] = piece[wide, table[0, o * SLOTS + k]]
+            to_first[wide, o] = piece[wide, table[0, o * SLOTS]]
 
         @pl.loop(1, REPS)
         def _(d):
-            owner(wide, d).start()
-
-        block_in[:, r, :, columns(wide)] = to_owner[wide, r]
-
-    def wait_route(wide):
-        landed(block_in.at[:, pl.ds(0, REPS - 1), :, columns(wide)], owner_r.at[wide])
+            owner_first(wide, d).start()
+
+        block_in[0, r, :, columns(wide)] = to_first[wide, r]
+
+    def route_second(turn):
+        each = BACK // WIDE
+
+        @pl.loop(0, REPS)
+        def _(o):
+            for i in range(each):
+                to_second[turn, o, :, pl.ds(i * WIDE, WIDE)] = (
+                    piece[turn * each + i, table[0, o * SLOTS + 1]])
+
+        @pl.loop(1, REPS)
+        def _(d):
+            owner_second(turn, d).start()
+
+        block_in[1, r, :, pl.ds(turn * BACK, BACK)] = to_second[turn, r]
+
+    def wait_first(wide):
+        landed(block_in.at[0, pl.ds(0, REPS - 1), :, columns(wide)], owner_r.at[wide])
+
+    def wait_second(turn):
+        landed(block_in.at[1, pl.ds(0, REPS - 1), :, pl.ds(turn * BACK, BACK)],
+               owner_r.at[STEPS + turn])
 
     roots = [pltpu.make_async_copy(ref, root_in.at[i], root_sem.at[i])
              for i, ref in enumerate((left_root, right_root))]
@@ -304,14 +329,18 @@
             root_hi[side, k, rows, :] = top
             root_lo[side, k, rows, :] = (whole - top.astype(f32)).astype(bf16)
 
+    combine(0)
+    start_near(1)
+    start_far(2)
+    for side in range(2):
+        split(side)
     for wide in range(STEPS):
-        combine(wide)
         if wide + 1 < STEPS:
-            start_near(wide + 1)
+            combine(wide + 1)
         if wide + 2 < STEPS:
-            start_far(wide + 2)
-        if wide < 2:
-            split(wide)
+            start_near(wide + 2)
+        if wide + 3 < STEPS:
+            start_far(wide + 3)
         if wide >= 1:
             line_combine(wide - 1)
         line_total(wide)
@@ -320,21 +349,28 @@
                 copy.start()
         if wide >= 1:
             total(wide - 1)
-            route(wide - 1)
+        if wide >= 2:
+            route_first(wide - 2)
+    route_first(STEPS - 2)
+    route_second(0)
     total(STEPS - 1)
-    route(STEPS - 1)
+    route_first(STEPS - 1)
 
     def square(d):
-        return send(squares, squares_in.at[d], square_s, square_r, other(d))
+        return send(squares_in.at[0], squares_in.at[d], square_s, square_r, other(d))
+
+    squares_in[0] = jnp.sum(squares[...], axis=0, keepdims=True)
 
     @pl.loop(1, REPS)
     def _(d):
         square(d).start()
 
-    def product(first, count):
-        @pl.loop(0, SLOTS * 2)
-        def _(i):
-            t, k = i // 2, i % 2
+    route_second(1)
+
+
+    def product(k, first, count):
+        @pl.loop(0, 2)
+        def _(t):
             rows = pl.ds(pl.multiple_of(t * 256, 256), 256)
             across = pl.ds(first, count)
             block = block_in[k, :, :, across].reshape(BLOCK, count)
@@ -346,52 +382,33 @@
             value = (jnp.dot(top, hi, preferred_element_type=f32)
                      + jnp.dot(top, lo, preferred_element_type=f32)
                      + jnp.dot(low, hi, preferred_element_type=f32))
-            if first == 0:
-                precond[k, rows, :] = value
-            else:
+            if first > 0:
                 value = precond[k, rows, :] + value
-                precond[k, rows, :] = value
+            precond[k, rows, :] = value
             if first + count == BLOCK:
                 ready[k, pl.ds(t * 8, 8)] = value.astype(bf16).reshape(8, PIECE, BLOCK)
 
-    def gather_column(d, value):
-        return value + squares_in[d]
-
     def column_in_root():
         return send(column.at[0], column_in.at[s], column_s, column_r, (ROOT, r))
 
     def column_out(d):
         return send(column.at[1], column_in.at[ROOT], column_s, column_r, ((ROOT + d) % COLS, r))
 
-    wait_route(0)
-    wait_route(1)
-    product(0, 2 * WIDE)
-    wait_route(2)
-    product(2 * WIDE, WIDE)
-
-    landed(squares_in.at[pl.ds(1, REPS - 1)], square_r)
-    all_squares = lax.fori_loop(1, REPS, gather_column, squares[...])
-    column[0] = jnp.sum(all_squares, axis=0, keepdims=True)
-
-    @pl.when(s != ROOT)
-    def _():
-        column_in_root().start()
-
-    wait_route(3)
-    product(3 * WIDE, WIDE)
-
-    def hold(turn, d):
-        return send(ready.at[:, (r + d) % REPS, :, pl.ds(turn * BACK, BACK)], held[turn].at[r],
-                    held_s, held_r.at[turn], other(d))
-
-    for turn in range(TURNS):
+    def hold_first(d):
+        return send(ready.at[0, peer(d)], held_first.at[r], held_s.at[0], held_r.at[TURNS], other(d))
+
+    def hold_second(turn, d):
+        return send(ready.at[1, peer(d), :, pl.ds(turn * BACK, BACK)], held[turn].at[r],
+                    held_s.at[1], held_r.at[turn], other(d))
+
+    def start_second(turn):
         @pl.loop(1, REPS)
         def _(d):
-            hold(turn, d).start()
-
-        held[turn][r] = ready[:, r, :, pl.ds(turn * BACK, BACK)]
-
-    for k in range(SLOTS):
+            hold_second(turn, d).start()
+
+        held[turn][r] = ready[1, r, :, pl.ds(turn * BACK, BACK)]
+
+    def graft(k):
         def square_sum(i, carry):
             value, power = carry
             p = precond[k, pl.ds(pl.multiple_of(i * PIECE, PIECE), PIECE), :]
@@ -408,11 +425,42 @@
     def scale_send(d):
         return send(scale_own, scale_in.at[r], scale_s, scale_r, other(d))
 
+    wait_first(0)
+    wait_first(1)
+    product(0, 0, 2 * WIDE)
+    wait_first(2)
+    product(0, 2 * WIDE, WIDE)
+    wait_second(0)
+    product(1, 0, BACK)
+    wait_first(3)
+    landed(squares_in.at[pl.ds(1, REPS - 1)], square_r)
+    column[0] = lax.fori_loop(1, REPS, lambda d, value: value + squares_in[d], squares_in[0])
+
+    @pl.when(s != ROOT)
+    def _():
+        column_in_root().start()
+
+    product(0, 3 * WIDE, WIDE)
+
+    @pl.loop(1, REPS)
+    def _(d):
+        hold_first(d).start()
+
+    held_first[r] = ready[0, r]
+    graft(0)
+
+    wait_second(1)
+    product(1, BACK, BACK)
+    start_second(0)
+    graft(1)
+
     @pl.loop(1, REPS)
     def _(d):
         scale_send(d).start()
 
     scale_in[r] = scale_own[...]
+    for turn in range(1, TURNS):
+        start_second(turn)
 
     @pl.when(s == ROOT)
     def _():
@@ -459,18 +507,21 @@
     landed(scale_in.at[pl.ds(0, REPS - 1)], scale_r)
 
     def settle(turn, d):
-        return send(to_place.at[turn, (r + d) % REPS], update.at[r, :, pl.ds(turn * BACK, BACK)],
+        return send(to_place.at[turn, peer(d)], update.at[r, :, pl.ds(turn * BACK, BACK)],
                     place_s, place_r, other(d))
 
     for turn in range(TURNS):
+        if turn == 0:
+            landed(held_first.at[pl.ds(0, REPS - 1)], held_r.at[TURNS])
         landed(held[turn].at[pl.ds(0, REPS - 1)], held_r.at[turn])
 
         @pl.loop(0, REPS)
         def _(j):
             o, k = table[1, j], table[2, j]
-            both_scales = scale_in[o]
-            scale = jnp.where(k == 0, both_scales[:1], both_scales[1:]) * clip
-            value = held[turn][o, k].astype(f32)
+            scales = scale_in[o]
+            scale = jnp.where(k == 0, scales[:1], scales[1:]) * clip
+            value = jnp.where(k == 0, held_first[o, :, pl.ds(turn * BACK, BACK)], held[turn][o])
+            value = value.astype(f32)
             for part in range(BACK // 128):
                 to_place[turn, j, :, pl.ds(part * 128, 128)] = (
                     value[:, part * 128:(part + 1) * 128] * scale).astype(bf16)
@@ -488,8 +539,10 @@
     left(line_far, lnear_s)
     left(line_far, lboth_s)
     left(line_in, line_s)
-    left(to_owner.at[:, pl.ds(0, REPS - 1)], owner_s)
-    left(ready.at[:, pl.ds(0, REPS - 1)], held_s)
+    left(to_first.at[:, pl.ds(0, REPS - 1)], owner_s.at[0])
+    left(to_second.at[:, pl.ds(0, REPS - 1)], owner_s.at[1])
+    left(ready.at[0, pl.ds(0, REPS - 1)], held_s.at[0])
+    left(ready.at[1, pl.ds(0, REPS - 1)], held_s.at[1])
     left(to_place.at[:, pl.ds(0, REPS - 1)], place_s)
     left(squares_in.at[pl.ds(1, REPS - 1)], square_s)
     left(scale_in.at[pl.ds(0, REPS - 1)], scale_s)
@@ -530,7 +583,8 @@
             pltpu.VMEM((lines, 2) + eighth, bf16),
             pltpu.VMEM((2, 3, REPS, HALF, WIDE), bf16),
             pltpu.VMEM((STEPS, REPS + 1, PIECE, WIDE), bf16),
-            pltpu.VMEM((STEPS, REPS, SLOTS, PIECE, WIDE), bf16),
+            pltpu.VMEM((STEPS, REPS, PIECE, WIDE), bf16),
+            pltpu.VMEM((TURNS, REPS, PIECE, BACK), bf16),
             pltpu.VMEM((SLOTS, REPS, PIECE, BLOCK), bf16),
             pltpu.VMEM((2, SLOTS, BLOCK, BLOCK), f32),
             pltpu.VMEM((2, SLOTS, BLOCK, BLOCK), bf16),
@@ -538,13 +592,14 @@
             pltpu.VMEM((2, SLOTS, BLOCK, BLOCK), f32),
             pltpu.VMEM((SLOTS, BLOCK, BLOCK), f32),
             pltpu.VMEM((SLOTS, REPS, PIECE, BLOCK), bf16),
-            pltpu.VMEM((REPS, SLOTS, PIECE, BACK), bf16),
-            pltpu.VMEM((REPS, SLOTS, PIECE, BACK), bf16),
+            pltpu.VMEM((REPS, PIECE, BLOCK), bf16),
+            pltpu.VMEM((REPS, PIECE, BACK), bf16),
+            pltpu.VMEM((REPS, PIECE, BACK), bf16),
             pltpu.VMEM((SLOTS, 128), f32),
             pltpu.VMEM((REPS, SLOTS, 128), f32),
             pltpu.VMEM((TURNS, REPS, PIECE, BACK), bf16),
             pltpu.VMEM((8, 128), f32),
-            pltpu.VMEM((REPS, 8, 128), f32),
+            pltpu.VMEM((REPS, 1, 128), f32),
             pltpu.VMEM((2, 1, 128), f32),
             pltpu.VMEM((COLS, 1, 128), f32),
             pltpu.SMEM((1, COLS * REPS), jnp.int32),
@@ -552,8 +607,8 @@
             dma((STEPS,)), dma((STEPS,)), dma((2,)), dma((2,)), dma,
             dma, dma((STEPS,)), dma, dma, dma((STEPS,)),
             dma, dma((STEPS - 1,)), dma, dma, dma((STEPS - 1,)),
-            dma, dma, dma, dma((STEPS,)),
-            dma, dma((TURNS,)), dma, dma, dma, dma,
+            dma, dma, dma((2,)), dma((STEPS + TURNS,)),
+            dma((2,)), dma((TURNS + 1,)), dma, dma, dma, dma,
             dma, dma, dma, dma,
         ],
         compiler_params=pltpu.CompilerParams(

time: 93.1 us -> 87.6 us (0.941)
  Pallas kernels: 88.9 us -> 83 us
    pallas_call x1, Pallas kernels: 88.9 us -> 83 us  [on_device(): pl.pallas_call(kernel, out_shape=(pltpu.VMEM((REPS, PIECE, BLOCK), bf16),...]
where the time goes in v4:
time: 87.6 us; the launch traced here: 87 us
  Pallas kernels  83 us (95%)
  local copies, waits for them, and re-layouts  3.43 us (4%)
    pallas_call x1, Pallas kernels, on_device(): pl.pallas_call(kernel, out_shape=(pltpu.VMEM((REPS, PIECE, BLOCK), bf16),...  83 us
    unnamed x3, local copies, waits for them, and re-layouts  3.43 us

profile of v4, /device:TPU:0, one launch (start us, length us, event | category | flops | bytes accessed | tf_op | source)
XLA Modules:
  0.0 87.0 jit_solution(11030464169491826107)
XLA Ops:
  0.6 83.0 %shard_map.85 = (bf16[16,32,512]{2,1,0:T(8,128)(2,1)S(1)}, f32[2,512,512]{2,1,0:T(8,128)S(1)}, f32[2,512,512]{2,1,0:T(8,128)S(1)}) custom-call(bf16[16,4,4,2,16,512]{5,4,3,2,1,0:T(8,128)(2,1)} %bitcast.12, s32[1,128]{1,0:T(1,128)} %bitcast.17, f32[2,512,512]{2,1,0:T(8,128)} %bitcast.13, f32[2,512,512]{2,1,0:T(8,128)} %bitcast.14, f32[2,512,512]{2,1,0:T(8,128)} %bitcast.15, ...), custom_call_target="tpu_custom_call" | custom-call | tf_op jit(solution)/shard_map/pallas_call | solution.py:571
  83.6 0.8 copy.12
  84.4 1.3 %copy.13 = f32[1,1,2,512,512]{4,3,2,1,0:T(8,128)} copy(f32[1,1,2,512,512]{4,3,2,1,0:T(8,128)S(1)} %bitcast.10) | data formatting | bytes 4194304
  85.7 1.3 %copy.14 = f32[1,1,2,512,512]{4,3,2,1,0:T(8,128)} copy(f32[1,1,2,512,512]{4,3,2,1,0:T(8,128)S(1)} %bitcast.9) | data formatting | bytes 4194304

commit v5 on v4

--- a/solution.py
+++ b/solution.py
@@ -53,7 +53,8 @@
         return (s, (y + step) % SIDE * SIDE + x)
 
     def peer(d):
-        return (r + d) % REPS
+        turned = d * 7 % REPS
+        return (y + turned // SIDE) % SIDE * SIDE + (x + turned % SIDE) % SIDE
 
     def other(d):
         return (s, peer(d))
@@ -332,6 +333,7 @@
     combine(0)
     start_near(1)
     start_far(2)
+    start_far(3)
     for side in range(2):
         split(side)
     for wide in range(STEPS):
@@ -339,11 +341,11 @@
             combine(wide + 1)
         if wide + 2 < STEPS:
             start_near(wide + 2)
-        if wide + 3 < STEPS:
-            start_far(wide + 3)
-        if wide >= 1:
+        if wide >= 1 and not direct(wide):
             line_combine(wide - 1)
         line_total(wide)
+        if direct(wide):
+            line_combine(wide - 1)
         if wide == 0:
             for copy in stats:
                 copy.start()
@@ -430,8 +432,6 @@
     product(0, 0, 2 * WIDE)
     wait_first(2)
     product(0, 2 * WIDE, WIDE)
-    wait_second(0)
-    product(1, 0, BACK)
     wait_first(3)
     landed(squares_in.at[pl.ds(1, REPS - 1)], square_r)
     column[0] = lax.fori_loop(1, REPS, lambda d, value: value + squares_in[d], squares_in[0])
@@ -447,11 +447,12 @@
         hold_first(d).start()
 
     held_first[r] = ready[0, r]
-    graft(0)
-
+    wait_second(0)
+    product(1, 0, BACK)
     wait_second(1)
     product(1, BACK, BACK)
     start_second(0)
+    graft(0)
     graft(1)
 
     @pl.loop(1, REPS)

time: 87.6 us -> 87.1 us (level)
  Pallas kernels: 83 us -> 81.9 us
    pallas_call x1, Pallas kernels: 83 us -> 81.9 us  [on_device(): pl.pallas_call(kernel, out_shape=(pltpu.VMEM((REPS, PIECE, BLOCK), bf16),...]
where the time goes in v5:
time: 87.1 us; the launch traced here: 85.9 us
  Pallas kernels  81.9 us (94%)
  local copies, waits for them, and re-layouts  3.43 us (4%)
    pallas_call x1, Pallas kernels, on_device(): pl.pallas_call(kernel, out_shape=(pltpu.VMEM((REPS, PIECE, BLOCK), bf16),...  81.9 us
    unnamed x3, local copies, waits for them, and re-layouts  3.43 us

profile of v5, /device:TPU:0, one launch (start us, length us, event | category | flops | bytes accessed | tf_op | source)
XLA Modules:
  0.0 85.9 jit_solution(11162959168535072947)
XLA Ops:
  0.6 81.9 %shard_map.85 = (bf16[16,32,512]{2,1,0:T(8,128)(2,1)S(1)}, f32[2,512,512]{2,1,0:T(8,128)S(1)}, f32[2,512,512]{2,1,0:T(8,128)S(1)}) custom-call(bf16[16,4,4,2,16,512]{5,4,3,2,1,0:T(8,128)(2,1)} %bitcast.12, s32[1,128]{1,0:T(1,128)} %bitcast.17, f32[2,512,512]{2,1,0:T(8,128)} %bitcast.13, f32[2,512,512]{2,1,0:T(8,128)} %bitcast.14, f32[2,512,512]{2,1,0:T(8,128)} %bitcast.15, ...), custom_call_target="tpu_custom_call" | custom-call | tf_op jit(solution)/shard_map/pallas_call | solution.py:572
  82.5 0.8 copy.12
  83.3 1.3 %copy.13 = f32[1,1,2,512,512]{4,3,2,1,0:T(8,128)} copy(f32[1,1,2,512,512]{4,3,2,1,0:T(8,128)S(1)} %bitcast.10) | data formatting | bytes 4194304
  84.6 1.3 %copy.14 = f32[1,1,2,512,512]{4,3,2,1,0:T(8,128)} copy(f32[1,1,2,512,512]{4,3,2,1,0:T(8,128)S(1)} %bitcast.9) | data formatting | bytes 4194304

commit v6 on v5

--- a/solution.py
+++ b/solution.py
@@ -163,7 +163,7 @@
         landed(far_in.at[pair(wide)], far_r.at[wide])
         for g in (2 * wide, 2 * wide + 1):
             for way in range(2):
-                @pl.loop(0, 8)
+                @pl.loop(0, 8, unroll=2)
                 def _(b):
                     near_own[g, way, b] = near_own[g, way, b] + far_in[g, way, b]
 
@@ -173,7 +173,7 @@
         loaded(last_own.at[pair(wide)], last_sem.at[wide])
         landed(pass_in.at[pair(wide)], pass_r.at[wide])
         for g in (2 * wide, 2 * wide + 1):
-            @pl.loop(0, 8)
+            @pl.loop(0, 8, unroll=2)
             def _(b):
                 for way in range(2):
                     total = (last_own[g, 8 * way + b].astype(f32)
@@ -196,7 +196,7 @@
             for way in range(2):
                 place = line_place(g, 1 - 2 * way)
 
-                @pl.loop(0, 8)
+                @pl.loop(0, 8, unroll=2)
                 def _(b):
                     line_sum[g, place, 8 * way + b] = (
                         line_sum[g, place, 8 * way + b] + line_far[g, way, b])
@@ -219,14 +219,14 @@
                 squares[...] += value[:8] + value[8:]
 
             if direct(wide):
-                @pl.loop(0, REPS)
+                @pl.loop(0, REPS, unroll=4)
                 def _(b):
                     value = line_sum[g, place, b].astype(f32)
                     for d in range(3):
                         value = value + line_in[g % 2, d, b].astype(f32)
                     finish(b, value)
             else:
-                @pl.loop(0, 8)
+                @pl.loop(0, 8, unroll=2)
                 def _(b):
                     for way in range(2):
                         finish(8 * way + b,
@@ -246,7 +246,7 @@
                     owner_s.at[1], owner_r.at[STEPS + turn], other(d))
 
     def route_first(wide):
-        @pl.loop(0, REPS)
+        @pl.loop(0, REPS, unroll=4)
         def _(o):
             to_first[wide, o] = piece[wide, table[0, o * SLOTS]]
 
@@ -259,7 +259,7 @@
     def route_second(turn):
         each = BACK // WIDE
 
-        @pl.loop(0, REPS)
+        @pl.loop(0, REPS, unroll=4)
         def _(o):
             for i in range(each):
                 to_second[turn, o, :, pl.ds(i * WIDE, WIDE)] = (
@@ -294,7 +294,7 @@
 
     names.wait()
 
-    @pl.loop(0, REPS)
+    @pl.loop(0, REPS, unroll=4)
     def _(j):
         mine = owners[0, s * REPS + j]
         count = jnp.int32(0)
@@ -304,7 +304,7 @@
         table[1, j] = mine
         table[2, j] = jnp.minimum(count, SLOTS - 1)
 
-    @pl.loop(0, REPS)
+    @pl.loop(0, REPS, unroll=4)
     def _(o):
         first, second = jnp.int32(REPS), jnp.int32(REPS)
         for j in range(REPS):
@@ -516,7 +516,7 @@
             landed(held_first.at[pl.ds(0, REPS - 1)], held_r.at[TURNS])
         landed(held[turn].at[pl.ds(0, REPS - 1)], held_r.at[turn])
 
-        @pl.loop(0, REPS)
+        @pl.loop(0, REPS, unroll=4)
         def _(j):
             o, k = table[1, j], table[2, j]
             scales = scale_in[o]

time: 87.1 us -> 86.9 us (level)
  no operation moved by 1% of the time
where the time goes in v6:
time: 86.9 us; the launch traced here: 85.8 us
  Pallas kernels  81.7 us (94%)
  local copies, waits for them, and re-layouts  3.43 us (4%)
    pallas_call x1, Pallas kernels, on_device(): pl.pallas_call(kernel, out_shape=(pltpu.VMEM((REPS, PIECE, BLOCK), bf16),...  81.7 us
    unnamed x3, local copies, waits for them, and re-layouts  3.43 us

profile of v6, /device:TPU:0, one launch (start us, length us, event | category | flops | bytes accessed | tf_op | source)
XLA Modules:
  0.0 85.8 jit_solution(17748826510379174178)
XLA Ops:
  0.6 81.7 %shard_map.85 = (bf16[16,32,512]{2,1,0:T(8,128)(2,1)S(1)}, f32[2,512,512]{2,1,0:T(8,128)S(1)}, f32[2,512,512]{2,1,0:T(8,128)S(1)}) custom-call(bf16[16,4,4,2,16,512]{5,4,3,2,1,0:T(8,128)(2,1)} %bitcast.12, s32[1,128]{1,0:T(1,128)} %bitcast.17, f32[2,512,512]{2,1,0:T(8,128)} %bitcast.13, f32[2,512,512]{2,1,0:T(8,128)} %bitcast.14, f32[2,512,512]{2,1,0:T(8,128)} %bitcast.15, ...), custom_call_target="tpu_custom_call" | custom-call | tf_op jit(solution)/shard_map/pallas_call | solution.py:572
  82.4 0.8 copy.12
  83.1 1.3 %copy.13 = f32[1,1,2,512,512]{4,3,2,1,0:T(8,128)} copy(f32[1,1,2,512,512]{4,3,2,1,0:T(8,128)S(1)} %bitcast.10) | data formatting | bytes 4194304
  84.5 1.3 %copy.14 = f32[1,1,2,512,512]{4,3,2,1,0:T(8,128)} copy(f32[1,1,2,512,512]{4,3,2,1,0:T(8,128)S(1)} %bitcast.9) | data formatting | bytes 4194304
